TPU v7x, 512 devices: a whole 4x8x8 slice. The times are simulated.
512 devices in a mesh: freq: 64 (over y, z_hi, x), bl: 8 (over z_lo, core).
Axes of the slice: x: 4, y: 8, z: 8 (z_hi: 2, z_lo: 4; z = z_hi * 4 + z_lo), core: 2. Of those that a mesh axis runs over, the one named last changes fastest.
Arguments:
- visibility_noise: float32 [128, 16, 2, 1024], P('freq', None, None, 'bl'), may hold values from -6 to 6
- baseline_wavelength_coords: float32 [3, 16, 1024], P(None, None, 'bl'), may hold values from -256 to 256
- station_pair: int32 [2, 1024], P(None, 'bl'), may hold values from 0 to 511, as said below
- comp_position: float32 [16, 2, 64], P('bl'), may hold values from -0.1 to 0.1
- comp_flux: float32 [16, 64], P('bl'), may hold values from 0.05 to 1
- comp_spectral: float32 [16, 64], P('bl'), may hold values from -1.5 to 0.5
- comp_count: int32 [16], P('bl'), may hold values from 1 to 64, 512 in all
- true_gains: float32 [128, 16, 2, 512], P('freq'), may hold values from 0.1 to 1.9
- start_gains: float32 [128, 16, 2, 512], P('freq'), may hold values from 0.1 to 1.9
- channel_flags: int32 [128], P('freq'), may hold values 0 or 1
Outputs:
- calibrated_gains: float32 [128, 16, 2, 512], P('freq')
- residual: float32 [128, 16, 2, 1024], P('freq', None, None, 'bl')
Inputs may be any that keep to these rules, and one draw needn't show every extreme that they name: `station_pair`: the two stations of a baseline differ. The first comp_count[d] slots of comp_position, comp_flux and comp_spectral of patch d are its components; the later slots are unused.
All inputs are finite; a program needn't handle non-finite values. No bound on the sum of `comp_count` or of `channel_flags` on one device may be relied on, other than what follows from the above.
Results may differ from a plain program's by a relative error of at most 0.0003.
Values sent between devices are 32-bit elements; how exact they have to be, the bound alone decides.
A program may use at most 64 MiB of HBM per device.

v0:
```python
import jax
import jax.numpy as jnp
from jax import lax
from jax.sharding import PartitionSpec as P

REACH = 4
ITERS = 3


TWO_PI = 6.283185307179586


def shifted(shard, axis, by):
    size = lax.axis_size(axis)
    pairs = [(i, i + by) for i in range(size) if 0 <= i + by < size]
    return lax.ppermute(shard, axis, pairs)


def channel_ratio(first_channel, channel_count, band_total):
    channel_ids = (first_channel + jnp.arange(channel_count)).astype(jnp.float32)
    return 0.5 + (channel_ids + 0.5) / band_total


def patch_model(position, fluxes, spectral, count_one, coords, ratios):
    block_size = 16
    log_ratio = jnp.log(ratios)
    block_turns = (count_one + block_size - 1) // block_size

    def add_block(turn_index, running):
        first_slot = turn_index * block_size
        eastward = lax.dynamic_slice_in_dim(position[0], first_slot, block_size, 0)
        northward = lax.dynamic_slice_in_dim(position[1], first_slot, block_size, 0)
        block_flux = lax.dynamic_slice_in_dim(fluxes, first_slot, block_size, 0)
        block_index = lax.dynamic_slice_in_dim(spectral, first_slot, block_size, 0)
        live_mask = (first_slot + jnp.arange(block_size) < count_one).astype(jnp.float32)
        depth_term = jnp.sqrt(1.0 - eastward * eastward - northward * northward) - 1.0
        spectrum = (block_flux * live_mask)[:, None] * jnp.exp(
            block_index[:, None] * log_ratio[None, :]
        )
        delays = (
            coords[0][None] * eastward[:, None, None]
            + coords[1][None] * northward[:, None, None]
            + coords[2][None] * depth_term[:, None, None]
        )
        phases = (TWO_PI * ratios)[None, :, None, None] * delays[:, None]
        weights = spectrum[:, :, None, None]
        real_part = jnp.sum(weights * jnp.cos(phases), axis=0)
        imag_part = -jnp.sum(weights * jnp.sin(phases), axis=0)
        return running + jnp.stack([real_part, imag_part], axis=2)

    initial = jnp.zeros((ratios.shape[0], coords.shape[1], 2, coords.shape[2]), jnp.float32)
    return lax.fori_loop(0, block_turns, add_block, initial)


def corrupt(gain_now, leading_station, second_station, sky_model):
    gain_first = jnp.take(gain_now, leading_station, axis=2)
    gain_second = jnp.take(gain_now, second_station, axis=2)
    joint_real = gain_first[:, 0] * gain_second[:, 0] + gain_first[:, 1] * gain_second[:, 1]
    joint_imag = gain_first[:, 1] * gain_second[:, 0] - gain_first[:, 0] * gain_second[:, 1]
    model_real = sky_model[:, :, 0]
    model_imag = sky_model[:, :, 1]
    term_real = joint_real[:, None] * model_real - joint_imag[:, None] * model_imag
    term_imag = joint_real[:, None] * model_imag + joint_imag[:, None] * model_real
    return (gain_first, gain_second, term_real, term_imag)


def observe(gain_now, leading_station, second_station, sky_model, noise_part):
    corrupted = corrupt(gain_now, leading_station, second_station, sky_model)
    return jnp.stack(
        [
            noise_part[:, 0] + jnp.sum(corrupted[2], axis=0),
            noise_part[:, 1] + jnp.sum(corrupted[3], axis=0),
        ],
        axis=1,
    )


def subtract_sky(gain_now, leading_station, second_station, sky_model, observed):
    corrupted = corrupt(gain_now, leading_station, second_station, sky_model)
    return jnp.stack(
        [
            observed[:, 0] - jnp.sum(corrupted[2], axis=0),
            observed[:, 1] - jnp.sum(corrupted[3], axis=0),
        ],
        axis=1,
    )


def station_terms(gain_now, leading_station, second_station, sky_model, observed):
    gain_first, gain_second, term_real, term_imag = corrupt(
        gain_now, leading_station, second_station, sky_model
    )
    rest_real = observed[:, 0] - jnp.sum(term_real, axis=0)
    rest_imag = observed[:, 1] - jnp.sum(term_imag, axis=0)
    single_real = rest_real[None] + term_real
    single_imag = rest_imag[None] + term_imag
    model_real = sky_model[:, :, 0]
    model_imag = sky_model[:, :, 1]
    fitted_real = jnp.sum(model_real * single_real + model_imag * single_imag, axis=1)
    fitted_imag = jnp.sum(model_real * single_imag - model_imag * single_real, axis=1)
    energy = jnp.sum(model_real * model_real + model_imag * model_imag, axis=1)
    first_real = gain_first[:, 0]
    first_imag = gain_first[:, 1]
    second_real = gain_second[:, 0]
    second_imag = gain_second[:, 1]
    toward_first = jnp.stack(
        [
            second_real * fitted_real - second_imag * fitted_imag,
            second_real * fitted_imag + second_imag * fitted_real,
            energy * (second_real * second_real + second_imag * second_imag),
        ],
        axis=1,
    )
    toward_second = jnp.stack(
        [
            first_real * fitted_real + first_imag * fitted_imag,
            first_imag * fitted_real - first_real * fitted_imag,
            energy * (first_real * first_real + first_imag * first_imag),
        ],
        axis=1,
    )
    return (toward_first, toward_second)


def collect(terms, onehot):
    flattened = terms.reshape(-1, terms.shape[3])
    summed = jnp.dot(flattened, onehot, precision=lax.Precision.HIGHEST)
    return summed.reshape(terms.shape[:3] + (onehot.shape[1],))


def update(gain_now, totals, weight):
    scaled = totals * weight[:, None, None, None]
    solved = scaled[:, :, 0:2] / jnp.maximum(scaled[:, :, 2:3], 1.0)
    return 0.5 * gain_now + 0.5 * solved


def kernel(shift_amounts, span):
    distance = shift_amounts.astype(jnp.float32)
    spread = 0.5 * span
    inside = (jnp.abs(shift_amounts) <= span).astype(jnp.float32)
    return jnp.exp(-(distance * distance) / (2.0 * spread * spread)) * inside


def smooth(mixed_gain, own_weight):
    channels_here = mixed_gain.shape[0]
    directions = mixed_gain.shape[1]
    span = REACH * channels_here
    local_terms = own_weight[:, None, None, None] * mixed_gain
    weight_slab = jnp.broadcast_to(
        own_weight[:, None, None, None],
        (channels_here, 1, mixed_gain.shape[2], mixed_gain.shape[3]),
    )
    packed = jnp.concatenate([local_terms, weight_slab], axis=1)
    row_ids = jnp.arange(channels_here)
    base_offsets = row_ids[:, None] - row_ids[None, :]

    def weigh_piece(device_offset, piece):
        matrix = kernel(device_offset * channels_here + base_offsets, span)
        flattened = piece.reshape(channels_here, -1)
        return jnp.dot(matrix, flattened, precision=lax.Precision.HIGHEST).reshape(piece.shape)

    summed = weigh_piece(0, packed)
    for distance in range(1, REACH + 1):
        from_below = shifted(packed, "freq", distance)
        from_above = shifted(packed, "freq", -distance)
        summed = summed + weigh_piece(distance, from_below) + weigh_piece(-distance, from_above)
    norm_sums = summed[:, directions, 0, 0]
    return summed[:, :directions] / jnp.maximum(norm_sums, 1.0)[:, None, None, None]


def local(
    visibility_noise,
    baseline_wavelength_coords,
    station_pair,
    comp_position,
    comp_flux,
    comp_spectral,
    comp_count,
    true_gains,
    start_gains,
    channel_flags,
):
    channels_here = visibility_noise.shape[0]
    stations = start_gains.shape[3]
    first_channel = lax.axis_index("freq") * channels_here
    ratios = channel_ratio(first_channel, channels_here, channels_here * lax.axis_size("freq"))
    weight = 1.0 - channel_flags.astype(jnp.float32)
    coords_all = lax.all_gather(baseline_wavelength_coords, "bl", axis=2, tiled=True)
    owned_model = jnp.stack(
        [
            patch_model(
                comp_position[patch_id],
                comp_flux[patch_id],
                comp_spectral[patch_id],
                comp_count[patch_id],
                coords_all,
                ratios,
            )
            for patch_id in range(comp_flux.shape[0])
        ],
        axis=1,
    )
    sky_model = lax.all_to_all(owned_model, "bl", split_axis=4, concat_axis=1, tiled=True)
    leading_station = station_pair[0]
    second_station = station_pair[1]
    station_ids = jnp.arange(stations)
    onehot_first = (leading_station[:, None] == station_ids[None, :]).astype(jnp.float32)
    onehot_second = (second_station[:, None] == station_ids[None, :]).astype(jnp.float32)
    observed = jax.vmap(observe, in_axes=(0, None, None, 0, 0))(
        true_gains, leading_station, second_station, sky_model, visibility_noise
    )
    gain_now = start_gains
    for iteration in range(ITERS):
        toward_first, toward_second = jax.vmap(station_terms, in_axes=(0, None, None, 0, 0))(
            gain_now, leading_station, second_station, sky_model, observed
        )
        partial_sums = collect(toward_first, onehot_first) + collect(toward_second, onehot_second)
        totals = lax.psum(partial_sums, "bl")
        gain_now = smooth(update(gain_now, totals, weight), weight)
    residual = jax.vmap(subtract_sky, in_axes=(0, None, None, 0, 0))(
        gain_now, leading_station, second_station, sky_model, observed
    )
    return (gain_now, residual)


def solution(mesh):
    in_specs = (
        P("freq", None, None, "bl"),
        P(None, None, "bl"),
        P(None, "bl"),
        P("bl", None, None),
        P("bl", None),
        P("bl", None),
        P("bl"),
        P("freq", None, None, None),
        P("freq", None, None, None),
        P("freq"),
    )
    out_specs = (P("freq", None, None, None), P("freq", None, None, "bl"))
    return jax.shard_map(local, mesh=mesh, in_specs=in_specs, out_specs=out_specs, check_vma=False)
```

profile of v0, /device:TPU:24, one launch (start us, length us, event | category | flops | bytes accessed | tf_op | source)
XLA Modules:
  0.0 623.2 jit_solution(505648292380763156)
XLA Ops:
  9.8 16.5 %all_gather.3 = f32[3,16,1024]{2,1,0:T(8,128)S(1)} all-gather(f32[3,16,128]{2,1,0:T(8,128)} %param.17), channel_id=1, replica_groups=mesh['freq'=64,'bl'=8] {'bl'}, dimensions={2}, use_global_device_ids=true | all-gather | bytes 221184 | tf_op jit(solution)/shard_map/all_gather | solution.py:188
  28.6 38.1 %while.29 = (s32[]{:T(128)}, f32[2,16,2,1024]{3,1,0,2:T(8,128)S(1)}, s32[]{:T(128)}, s32[]{:T(128)}, f32[64]{0:T(128)S(1)}, /*index=5*/f32[64]{0:T(128)S(1)}, f3...) while((s32[]{:T(128)}, ...), condition=%wide.region_7.9_spmd.clone.clone, body=%wide.region_4.8_spmd.clone.clone.sunk | while | flops 4030674 | bytes 4000095 | solution.py:52
  29.8 8.2 %fusion.366 = (f32[2,16,1024]{2,1,0:T(8,128)S(1)}, f32[2,16,1024]{2,1,0:T(8,128)S(1)}) fusion(f32[16,16,1024]{2,1,0:T(8,128)S(1)} %multiply_add_fusion.12, f32[2]{0:T(128)S(1)} %get-tuple-element.675, f32[16,2]{1,0:T(8,128)S(1)} %exponential_multiply_fusion.5), kind=kLoop, calls=%fused_computation.37.clone.1 | loop fusion | flops 2555904 | bytes 1310856 | tf_op jit(solution)/shard_map/while/body/reduce_sum | solution.py:47
  39.3 8.2 %fusion.366 = (f32[2,16,1024]{2,1,0:T(8,128)S(1)}, f32[2,16,1024]{2,1,0:T(8,128)S(1)}) fusion(f32[16,16,1024]{2,1,0:T(8,128)S(1)} %multiply_add_fusion.12, f32[2]{0:T(128)S(1)} %get-tuple-element.675, f32[16,2]{1,0:T(8,128)S(1)} %exponential_multiply_fusion.5), kind=kLoop, calls=%fused_computation.37.clone.1 | loop fusion | flops 2555904 | bytes 1310856 | tf_op jit(solution)/shard_map/while/body/reduce_sum | solution.py:47
  48.9 8.2 %fusion.366 = (f32[2,16,1024]{2,1,0:T(8,128)S(1)}, f32[2,16,1024]{2,1,0:T(8,128)S(1)}) fusion(f32[16,16,1024]{2,1,0:T(8,128)S(1)} %multiply_add_fusion.12, f32[2]{0:T(128)S(1)} %get-tuple-element.675, f32[16,2]{1,0:T(8,128)S(1)} %exponential_multiply_fusion.5), kind=kLoop, calls=%fused_computation.37.clone.1 | loop fusion | flops 2555904 | bytes 1310856 | tf_op jit(solution)/shard_map/while/body/reduce_sum | solution.py:47
  58.4 8.2 %fusion.366 = (f32[2,16,1024]{2,1,0:T(8,128)S(1)}, f32[2,16,1024]{2,1,0:T(8,128)S(1)}) fusion(f32[16,16,1024]{2,1,0:T(8,128)S(1)} %multiply_add_fusion.12, f32[2]{0:T(128)S(1)} %get-tuple-element.675, f32[16,2]{1,0:T(8,128)S(1)} %exponential_multiply_fusion.5), kind=kLoop, calls=%fused_computation.37.clone.1 | loop fusion | flops 2555904 | bytes 1310856 | tf_op jit(solution)/shard_map/while/body/reduce_sum | solution.py:47
  66.8 28.8 %while.28 = (s32[]{:T(128)}, f32[2,16,2,1024]{3,1,0,2:T(8,128)S(1)}, s32[]{:T(128)}, s32[]{:T(128)}, f32[64]{0:T(128)S(1)}, /*index=5*/f32[64]{0:T(128)S(1)}, f3...) while((s32[]{:T(128)}, ...), condition=%wide.region_3.5_spmd.clone.clone, body=%wide.region_0.4_spmd.clone.clone.sunk | while | flops 4030674 | bytes 4000095 | solution.py:52
  68.1 8.3 %fusion.363 = (f32[2,16,1024]{2,1,0:T(8,128)S(1)}, f32[2,16,1024]{2,1,0:T(8,128)S(1)}) fusion(f32[16,16,1024]{2,1,0:T(8,128)S(1)} %multiply_add_fusion.11, f32[2]{0:T(128)S(1)} %get-tuple-element.653, f32[16,2]{1,0:T(8,128)S(1)} %exponential_multiply_fusion.4), kind=kLoop, calls=%fused_computation.17.clone.1 | loop fusion | flops 2555904 | bytes 1310856 | tf_op jit(solution)/shard_map/while/body/reduce_sum | solution.py:47
  77.6 8.3 %fusion.363 = (f32[2,16,1024]{2,1,0:T(8,128)S(1)}, f32[2,16,1024]{2,1,0:T(8,128)S(1)}) fusion(f32[16,16,1024]{2,1,0:T(8,128)S(1)} %multiply_add_fusion.11, f32[2]{0:T(128)S(1)} %get-tuple-element.653, f32[16,2]{1,0:T(8,128)S(1)} %exponential_multiply_fusion.4), kind=kLoop, calls=%fused_computation.17.clone.1 | loop fusion | flops 2555904 | bytes 1310856 | tf_op jit(solution)/shard_map/while/body/reduce_sum | solution.py:47
  87.2 8.3 %fusion.363 = (f32[2,16,1024]{2,1,0:T(8,128)S(1)}, f32[2,16,1024]{2,1,0:T(8,128)S(1)}) fusion(f32[16,16,1024]{2,1,0:T(8,128)S(1)} %multiply_add_fusion.11, f32[2]{0:T(128)S(1)} %get-tuple-element.653, f32[16,2]{1,0:T(8,128)S(1)} %exponential_multiply_fusion.4), kind=kLoop, calls=%fused_computation.17.clone.1 | loop fusion | flops 2555904 | bytes 1310856 | tf_op jit(solution)/shard_map/while/body/reduce_sum | solution.py:47
  95.7 4.3 copy.385
  100.0 7.9 %reshape.589 = f32[8,1,16384]{2,1,0:T(1,128)} reshape(f32[1024,2,2,2,16]{4,3,2,1,0:T(2,128)} %bitcast.480) | data formatting | bytes 1048576
  107.9 12.9 %all-to-all-start = ((f32[8,1,16384]{2,1,0:T(1,128)}), f32[8,1,16384]{2,1,0:T(1,128)S(1)}, u32[]{:S(2)}, u32[]{:S(2)}) async-start(f32[8,1,16384]{2,1,0:T(1,128)} %reshape.589), calls=%async_computation | async-start | bytes 1048576 | tf_op jit(solution)/shard_map/all_to_all | solution.py:203
  127.3 8.9 %all-to-all-done = f32[8,1,16384]{2,1,0:T(1,128)S(1)} async-done(((f32[8,1,16384]{2,1,0:T(1,128)}), f32[8,1,16384]{2,1,0:T(1,128)S(1)}, u32[]{:S(2)}, u32[]{:S(2)}) %all-to-all-start) | async-done | bytes 524320 | tf_op jit(solution)/shard_map/all_to_all | solution.py:203
  136.7 1.9 reduce.6
  138.6 7.5 %reshape.590 = f32[1024,2,2,2,16]{4,3,2,1,0:T(2,128)} reshape(f32[8,16384]{1,0:T(8,128)S(1)} %reduce.6) | data formatting | bytes 1048576
  146.1 5.1 copy.479
  151.3 5.1 copy.480
  158.3 78.1 %all-reduce.4.cloned.1.call-done = f32[2,16,3,512]{3,1,2,0:T(8,128)} async-done(((f32[2,16,3,512]{3,1,2,0:T(8,128)}), f32[2,16,3,512]{3,1,2,0:T(8,128)}) %all-reduce.4.cloned.1.call-update) | async-done | bytes 196624 | tf_op jit(solution)/shard_map/psum | solution.py:218
  237.6 5.3 collective-permute-start.7
  242.9 4.5 collective-permute-start.6
  247.4 7.1 %collective-permute-start.5 = (f32[2,17,2,512]{3,1,2,0:T(8,128)S(1)}, f32[2,17,2,512]{3,1,2,0:T(8,128)S(1)}, u32[]{:S(2)}, u32[]{:S(2)}) collective-permute-start(f32[2,17,2,512]{3,1,2,0:T(8,128)S(1)} %pad_maximum_fusion.3), channel_id=1, source_target_pairs={{24,0},{32,8},{40,16},{48,24},{56,32},{64,40},{72,48},{80,56},{88,... | collective-permute-start | bytes 417800 | tf_op jit(solution)/shard_map/ppermute | solution.py:16
  254.5 1.9 collective-permute-start.4
  256.4 11.1 %collective-permute-start.3 = (f32[2,17,2,512]{3,1,2,0:T(8,128)S(1)}, f32[2,17,2,512]{3,1,2,0:T(8,128)S(1)}, u32[]{:S(2)}, u32[]{:S(2)}) collective-permute-start(f32[2,17,2,512]{3,1,2,0:T(8,128)S(1)} %pad_maximum_fusion.3), channel_id=1, source_target_pairs={{16,0},{24,8},{32,16},{40,24},{48,32},{56,40},{64,48},{72,56},{80,... | collective-permute-start | bytes 417800 | tf_op jit(solution)/shard_map/ppermute | solution.py:16
  268.5 21.7 %collective-permute-start.2 = (f32[2,17,2,512]{3,1,2,0:T(8,128)S(1)}, f32[2,17,2,512]{3,1,2,0:T(8,128)S(1)}, u32[]{:S(2)}, u32[]{:S(2)}) collective-permute-start(f32[2,17,2,512]{3,1,2,0:T(8,128)S(1)} %pad_maximum_fusion.3), channel_id=1, source_target_pairs={{0,16},{8,24},{16,32},{24,40},{32,48},{40,56},{48,64},{56,72},{64,... | collective-permute-start | bytes 417800 | tf_op jit(solution)/shard_map/ppermute | solution.py:16
  291.1 2.1 collective-permute-start.1
  294.1 3.9 collective-permute-start
  302.6 6.0 collective-permute-done
  314.6 72.6 %all-reduce.6.cloned.1.call-done = f32[2,16,3,512]{3,1,2,0:T(8,128)} async-done(((f32[2,16,3,512]{3,1,2,0:T(8,128)}), f32[2,16,3,512]{3,1,2,0:T(8,128)}) %all-reduce.6.cloned.1.call-update) | async-done | bytes 196624 | tf_op jit(solution)/shard_map/psum | solution.py:218
  388.3 5.3 collective-permute-start.15
  393.6 4.5 collective-permute-start.14
  398.1 7.1 %collective-permute-start.13 = (f32[2,17,2,512]{3,1,2,0:T(8,128)S(1)}, f32[2,17,2,512]{3,1,2,0:T(8,128)S(1)}, u32[]{:S(2)}, u32[]{:S(2)}) collective-permute-start(f32[2,17,2,512]{3,1,2,0:T(8,128)S(1)} %pad_maximum_fusion.2), channel_id=1, source_target_pairs={{24,0},{32,8},{40,16},{48,24},{56,32},{64,40},{72,48},{80,56},{88,... | collective-permute-start | bytes 417800 | tf_op jit(solution)/shard_map/ppermute | solution.py:16
  405.2 1.9 collective-permute-start.12
  407.1 11.1 %collective-permute-start.11 = (f32[2,17,2,512]{3,1,2,0:T(8,128)S(1)}, f32[2,17,2,512]{3,1,2,0:T(8,128)S(1)}, u32[]{:S(2)}, u32[]{:S(2)}) collective-permute-start(f32[2,17,2,512]{3,1,2,0:T(8,128)S(1)} %pad_maximum_fusion.2), channel_id=1, source_target_pairs={{16,0},{24,8},{32,16},{40,24},{48,32},{56,40},{64,48},{72,56},{80,... | collective-permute-start | bytes 417800 | tf_op jit(solution)/shard_map/ppermute | solution.py:16
  419.2 21.7 %collective-permute-start.10 = (f32[2,17,2,512]{3,1,2,0:T(8,128)S(1)}, f32[2,17,2,512]{3,1,2,0:T(8,128)S(1)}, u32[]{:S(2)}, u32[]{:S(2)}) collective-permute-start(f32[2,17,2,512]{3,1,2,0:T(8,128)S(1)} %pad_maximum_fusion.2), channel_id=1, source_target_pairs={{0,16},{8,24},{16,32},{24,40},{32,48},{40,56},{48,64},{56,72},{64,... | collective-permute-start | bytes 417800 | tf_op jit(solution)/shard_map/ppermute | solution.py:16
  441.8 2.3 collective-permute-start.9
  445.1 3.9 collective-permute-start.8
  453.6 6.0 collective-permute-done.8
  465.5 72.7 %all-reduce.8.cloned.1.call-done = f32[2,16,3,512]{3,1,2,0:T(8,128)} async-done(((f32[2,16,3,512]{3,1,2,0:T(8,128)}), f32[2,16,3,512]{3,1,2,0:T(8,128)}) %all-reduce.8.cloned.1.call-update) | async-done | bytes 196624 | tf_op jit(solution)/shard_map/psum | solution.py:218
  539.3 5.3 collective-permute-start.23
  544.6 4.5 collective-permute-start.22
  549.0 7.1 %collective-permute-start.21 = (f32[2,17,2,512]{3,1,2,0:T(8,128)S(1)}, f32[2,17,2,512]{3,1,2,0:T(8,128)S(1)}, u32[]{:S(2)}, u32[]{:S(2)}) collective-permute-start(f32[2,17,2,512]{3,1,2,0:T(8,128)S(1)} %pad_maximum_fusion.1), channel_id=1, source_target_pairs={{24,0},{32,8},{40,16},{48,24},{56,32},{64,40},{72,48},{80,56},{88,... | collective-permute-start | bytes 417800 | tf_op jit(solution)/shard_map/ppermute | solution.py:16
  556.1 1.9 collective-permute-start.20
  558.1 11.1 %collective-permute-start.19 = (f32[2,17,2,512]{3,1,2,0:T(8,128)S(1)}, f32[2,17,2,512]{3,1,2,0:T(8,128)S(1)}, u32[]{:S(2)}, u32[]{:S(2)}) collective-permute-start(f32[2,17,2,512]{3,1,2,0:T(8,128)S(1)} %pad_maximum_fusion.1), channel_id=1, source_target_pairs={{16,0},{24,8},{32,16},{40,24},{48,32},{56,40},{64,48},{72,56},{80,... | collective-permute-start | bytes 417800 | tf_op jit(solution)/shard_map/ppermute | solution.py:16
  570.1 21.7 %collective-permute-start.18 = (f32[2,17,2,512]{3,1,2,0:T(8,128)S(1)}, f32[2,17,2,512]{3,1,2,0:T(8,128)S(1)}, u32[]{:S(2)}, u32[]{:S(2)}) collective-permute-start(f32[2,17,2,512]{3,1,2,0:T(8,128)S(1)} %pad_maximum_fusion.1), channel_id=1, source_target_pairs={{0,16},{8,24},{16,32},{24,40},{32,48},{40,56},{48,64},{56,72},{64,... | collective-permute-start | bytes 417800 | tf_op jit(solution)/shard_map/ppermute | solution.py:16
  592.7 2.1 collective-permute-start.17
  595.8 3.9 collective-permute-start.16
  604.2 6.0 collective-permute-done.16
  (283 shorter events, 63.5 us)
Async XLA Ops:
  100.0 21.1 %copy-start.3 = (s32[2,128]{1,0:T(2,128)S(1)}, s32[2,128]{1,0:T(2,128)}, u32[]{:S(2)}) copy-start(s32[2,128]{1,0:T(2,128)} %param.18) | copy-start | bytes 3076
  100.0 21.1 %copy-start.1 = (f32[2,16,2,512]{3,2,1,0:T(2,128)S(1)}, f32[2,16,2,512]{3,2,1,0:T(2,128)}, u32[]{:S(2)}) copy-start(f32[2,16,2,512]{3,2,1,0:T(2,128)} %param.23) | copy-start | bytes 393220
  107.9 16.4 %copy-start = (f32[2,16,2,512]{3,2,1,0:T(2,128)S(1)}, f32[2,16,2,512]{3,2,1,0:T(2,128)}, u32[]{:S(2)}) copy-start(f32[2,16,2,512]{3,2,1,0:T(2,128)} %param.24) | copy-start | bytes 393220
  107.9 28.3 %all-to-all-start = ((f32[8,1,16384]{2,1,0:T(1,128)}), f32[8,1,16384]{2,1,0:T(1,128)S(1)}, u32[]{:S(2)}, u32[]{:S(2)}) async-start(f32[8,1,16384]{2,1,0:T(1,128)} %reshape.589), calls=%async_computation | async-start | bytes 1048576 | tf_op jit(solution)/shard_map/all_to_all | solution.py:203
  120.9 115.5 %all-reduce.4.cloned.1.call-start = ((), (), s32[]{:S(2)}) async-start(), calls=%async_computation.1 | async-start | bytes 393216 | tf_op jit(solution)/shard_map/psum | solution.py:218
  121.7 5.5 copy-start.2
  156.4 1.9 copy-start.4
  158.2 228.9 %all-reduce.6.cloned.1.call-start = ((), (), s32[]{:S(2)}) async-start(), calls=%async_computation.2 | async-start | bytes 393216 | tf_op jit(solution)/shard_map/psum | solution.py:218
  237.6 30.9 %collective-permute-start.7 = (f32[2,17,2,512]{3,1,2,0:T(8,128)S(1)}, f32[2,17,2,512]{3,1,2,0:T(8,128)S(1)}, u32[]{:S(2)}, u32[]{:S(2)}) collective-permute-start(f32[2,17,2,512]{3,1,2,0:T(8,128)S(1)} %pad_maximum_fusion.3), channel_id=1, source_target_pairs={{32,0},{40,8},{48,16},{56,24},{64,32},{72,40},{80,48},{88,56},{96,... | collective-permute-start | bytes 417800 | tf_op jit(solution)/shard_map/ppermute | solution.py:16
  242.9 48.2 %collective-permute-start.6 = (f32[2,17,2,512]{3,1,2,0:T(8,128)S(1)}, f32[2,17,2,512]{3,1,2,0:T(8,128)S(1)}, u32[]{:S(2)}, u32[]{:S(2)}) collective-permute-start(f32[2,17,2,512]{3,1,2,0:T(8,128)S(1)} %pad_maximum_fusion.3), channel_id=1, source_target_pairs={{0,32},{8,40},{16,48},{24,56},{32,64},{40,72},{48,80},{56,88},{64,... | collective-permute-start | bytes 417800 | tf_op jit(solution)/shard_map/ppermute | solution.py:16
  247.4 46.7 %collective-permute-start.5 = (f32[2,17,2,512]{3,1,2,0:T(8,128)S(1)}, f32[2,17,2,512]{3,1,2,0:T(8,128)S(1)}, u32[]{:S(2)}, u32[]{:S(2)}) collective-permute-start(f32[2,17,2,512]{3,1,2,0:T(8,128)S(1)} %pad_maximum_fusion.3), channel_id=1, source_target_pairs={{24,0},{32,8},{40,16},{48,24},{56,32},{64,40},{72,48},{80,56},{88,... | collective-permute-start | bytes 417800 | tf_op jit(solution)/shard_map/ppermute | solution.py:16
  254.5 44.5 %collective-permute-start.4 = (f32[2,17,2,512]{3,1,2,0:T(8,128)S(1)}, f32[2,17,2,512]{3,1,2,0:T(8,128)S(1)}, u32[]{:S(2)}, u32[]{:S(2)}) collective-permute-start(f32[2,17,2,512]{3,1,2,0:T(8,128)S(1)} %pad_maximum_fusion.3), channel_id=1, source_target_pairs={{0,24},{8,32},{16,40},{24,48},{32,56},{40,64},{48,72},{56,80},{64,... | collective-permute-start | bytes 417800 | tf_op jit(solution)/shard_map/ppermute | solution.py:16
  256.4 43.5 %collective-permute-start.3 = (f32[2,17,2,512]{3,1,2,0:T(8,128)S(1)}, f32[2,17,2,512]{3,1,2,0:T(8,128)S(1)}, u32[]{:S(2)}, u32[]{:S(2)}) collective-permute-start(f32[2,17,2,512]{3,1,2,0:T(8,128)S(1)} %pad_maximum_fusion.3), channel_id=1, source_target_pairs={{16,0},{24,8},{32,16},{40,24},{48,32},{56,40},{64,48},{72,56},{80,... | collective-permute-start | bytes 417800 | tf_op jit(solution)/shard_map/ppermute | solution.py:16
  268.5 32.3 %collective-permute-start.2 = (f32[2,17,2,512]{3,1,2,0:T(8,128)S(1)}, f32[2,17,2,512]{3,1,2,0:T(8,128)S(1)}, u32[]{:S(2)}, u32[]{:S(2)}) collective-permute-start(f32[2,17,2,512]{3,1,2,0:T(8,128)S(1)} %pad_maximum_fusion.3), channel_id=1, source_target_pairs={{0,16},{8,24},{16,32},{24,40},{32,48},{40,56},{48,64},{56,72},{64,... | collective-permute-start | bytes 417800 | tf_op jit(solution)/shard_map/ppermute | solution.py:16
  291.1 10.6 %collective-permute-start.1 = (f32[2,17,2,512]{3,1,2,0:T(8,128)S(1)}, f32[2,17,2,512]{3,1,2,0:T(8,128)S(1)}, u32[]{:S(2)}, u32[]{:S(2)}) collective-permute-start(f32[2,17,2,512]{3,1,2,0:T(8,128)S(1)} %pad_maximum_fusion.3), channel_id=1, source_target_pairs={{8,0},{16,8},{24,16},{32,24},{40,32},{48,40},{56,48},{64,56},{72,6... | collective-permute-start | bytes 417800 | tf_op jit(solution)/shard_map/ppermute | solution.py:16
  294.1 14.5 %collective-permute-start = (f32[2,17,2,512]{3,1,2,0:T(8,128)S(1)}, f32[2,17,2,512]{3,1,2,0:T(8,128)S(1)}, u32[]{:S(2)}, u32[]{:S(2)}) collective-permute-start(f32[2,17,2,512]{3,1,2,0:T(8,128)S(1)} %pad_maximum_fusion.3), channel_id=1, source_target_pairs={{0,8},{8,16},{16,24},{24,32},{32,40},{40,48},{48,56},{56,64},{64,7... | collective-permute-start | bytes 417800 | tf_op jit(solution)/shard_map/ppermute | solution.py:16
  314.5 223.6 %all-reduce.8.cloned.1.call-start = ((), (), s32[]{:S(2)}) async-start(), calls=%async_computation.3 | async-start | bytes 393216 | tf_op jit(solution)/shard_map/psum | solution.py:218
  388.3 30.9 %collective-permute-start.15 = (f32[2,17,2,512]{3,1,2,0:T(8,128)S(1)}, f32[2,17,2,512]{3,1,2,0:T(8,128)S(1)}, u32[]{:S(2)}, u32[]{:S(2)}) collective-permute-start(f32[2,17,2,512]{3,1,2,0:T(8,128)S(1)} %pad_maximum_fusion.2), channel_id=1, source_target_pairs={{32,0},{40,8},{48,16},{56,24},{64,32},{72,40},{80,48},{88,56},{96,... | collective-permute-start | bytes 417800 | tf_op jit(solution)/shard_map/ppermute | solution.py:16
  393.6 48.2 %collective-permute-start.14 = (f32[2,17,2,512]{3,1,2,0:T(8,128)S(1)}, f32[2,17,2,512]{3,1,2,0:T(8,128)S(1)}, u32[]{:S(2)}, u32[]{:S(2)}) collective-permute-start(f32[2,17,2,512]{3,1,2,0:T(8,128)S(1)} %pad_maximum_fusion.2), channel_id=1, source_target_pairs={{0,32},{8,40},{16,48},{24,56},{32,64},{40,72},{48,80},{56,88},{64,... | collective-permute-start | bytes 417800 | tf_op jit(solution)/shard_map/ppermute | solution.py:16
  398.1 46.9 %collective-permute-start.13 = (f32[2,17,2,512]{3,1,2,0:T(8,128)S(1)}, f32[2,17,2,512]{3,1,2,0:T(8,128)S(1)}, u32[]{:S(2)}, u32[]{:S(2)}) collective-permute-start(f32[2,17,2,512]{3,1,2,0:T(8,128)S(1)} %pad_maximum_fusion.2), channel_id=1, source_target_pairs={{24,0},{32,8},{40,16},{48,24},{56,32},{64,40},{72,48},{80,56},{88,... | collective-permute-start | bytes 417800 | tf_op jit(solution)/shard_map/ppermute | solution.py:16
  405.2 44.7 %collective-permute-start.12 = (f32[2,17,2,512]{3,1,2,0:T(8,128)S(1)}, f32[2,17,2,512]{3,1,2,0:T(8,128)S(1)}, u32[]{:S(2)}, u32[]{:S(2)}) collective-permute-start(f32[2,17,2,512]{3,1,2,0:T(8,128)S(1)} %pad_maximum_fusion.2), channel_id=1, source_target_pairs={{0,24},{8,32},{16,40},{24,48},{32,56},{40,64},{48,72},{56,80},{64,... | collective-permute-start | bytes 417800 | tf_op jit(solution)/shard_map/ppermute | solution.py:16
  407.1 43.7 %collective-permute-start.11 = (f32[2,17,2,512]{3,1,2,0:T(8,128)S(1)}, f32[2,17,2,512]{3,1,2,0:T(8,128)S(1)}, u32[]{:S(2)}, u32[]{:S(2)}) collective-permute-start(f32[2,17,2,512]{3,1,2,0:T(8,128)S(1)} %pad_maximum_fusion.2), channel_id=1, source_target_pairs={{16,0},{24,8},{32,16},{40,24},{48,32},{56,40},{64,48},{72,56},{80,... | collective-permute-start | bytes 417800 | tf_op jit(solution)/shard_map/ppermute | solution.py:16
  419.2 32.5 %collective-permute-start.10 = (f32[2,17,2,512]{3,1,2,0:T(8,128)S(1)}, f32[2,17,2,512]{3,1,2,0:T(8,128)S(1)}, u32[]{:S(2)}, u32[]{:S(2)}) collective-permute-start(f32[2,17,2,512]{3,1,2,0:T(8,128)S(1)} %pad_maximum_fusion.2), channel_id=1, source_target_pairs={{0,16},{8,24},{16,32},{24,40},{32,48},{40,56},{48,64},{56,72},{64,... | collective-permute-start | bytes 417800 | tf_op jit(solution)/shard_map/ppermute | solution.py:16
  441.8 10.8 %collective-permute-start.9 = (f32[2,17,2,512]{3,1,2,0:T(8,128)S(1)}, f32[2,17,2,512]{3,1,2,0:T(8,128)S(1)}, u32[]{:S(2)}, u32[]{:S(2)}) collective-permute-start(f32[2,17,2,512]{3,1,2,0:T(8,128)S(1)} %pad_maximum_fusion.2), channel_id=1, source_target_pairs={{8,0},{16,8},{24,16},{32,24},{40,32},{48,40},{56,48},{64,56},{72,6... | collective-permute-start | bytes 417800 | tf_op jit(solution)/shard_map/ppermute | solution.py:16
  445.1 14.5 %collective-permute-start.8 = (f32[2,17,2,512]{3,1,2,0:T(8,128)S(1)}, f32[2,17,2,512]{3,1,2,0:T(8,128)S(1)}, u32[]{:S(2)}, u32[]{:S(2)}) collective-permute-start(f32[2,17,2,512]{3,1,2,0:T(8,128)S(1)} %pad_maximum_fusion.2), channel_id=1, source_target_pairs={{0,8},{8,16},{16,24},{24,32},{32,40},{40,48},{48,56},{56,64},{64,7... | collective-permute-start | bytes 417800 | tf_op jit(solution)/shard_map/ppermute | solution.py:16
  539.3 30.9 %collective-permute-start.23 = (f32[2,17,2,512]{3,1,2,0:T(8,128)S(1)}, f32[2,17,2,512]{3,1,2,0:T(8,128)S(1)}, u32[]{:S(2)}, u32[]{:S(2)}) collective-permute-start(f32[2,17,2,512]{3,1,2,0:T(8,128)S(1)} %pad_maximum_fusion.1), channel_id=1, source_target_pairs={{32,0},{40,8},{48,16},{56,24},{64,32},{72,40},{80,48},{88,56},{96,... | collective-permute-start | bytes 417800 | tf_op jit(solution)/shard_map/ppermute | solution.py:16
  544.6 48.2 %collective-permute-start.22 = (f32[2,17,2,512]{3,1,2,0:T(8,128)S(1)}, f32[2,17,2,512]{3,1,2,0:T(8,128)S(1)}, u32[]{:S(2)}, u32[]{:S(2)}) collective-permute-start(f32[2,17,2,512]{3,1,2,0:T(8,128)S(1)} %pad_maximum_fusion.1), channel_id=1, source_target_pairs={{0,32},{8,40},{16,48},{24,56},{32,64},{40,72},{48,80},{56,88},{64,... | collective-permute-start | bytes 417800 | tf_op jit(solution)/shard_map/ppermute | solution.py:16
  549.0 46.7 %collective-permute-start.21 = (f32[2,17,2,512]{3,1,2,0:T(8,128)S(1)}, f32[2,17,2,512]{3,1,2,0:T(8,128)S(1)}, u32[]{:S(2)}, u32[]{:S(2)}) collective-permute-start(f32[2,17,2,512]{3,1,2,0:T(8,128)S(1)} %pad_maximum_fusion.1), channel_id=1, source_target_pairs={{24,0},{32,8},{40,16},{48,24},{56,32},{64,40},{72,48},{80,56},{88,... | collective-permute-start | bytes 417800 | tf_op jit(solution)/shard_map/ppermute | solution.py:16
  556.1 44.4 %collective-permute-start.20 = (f32[2,17,2,512]{3,1,2,0:T(8,128)S(1)}, f32[2,17,2,512]{3,1,2,0:T(8,128)S(1)}, u32[]{:S(2)}, u32[]{:S(2)}) collective-permute-start(f32[2,17,2,512]{3,1,2,0:T(8,128)S(1)} %pad_maximum_fusion.1), channel_id=1, source_target_pairs={{0,24},{8,32},{16,40},{24,48},{32,56},{40,64},{48,72},{56,80},{64,... | collective-permute-start | bytes 417800 | tf_op jit(solution)/shard_map/ppermute | solution.py:16
  558.1 43.4 %collective-permute-start.19 = (f32[2,17,2,512]{3,1,2,0:T(8,128)S(1)}, f32[2,17,2,512]{3,1,2,0:T(8,128)S(1)}, u32[]{:S(2)}, u32[]{:S(2)}) collective-permute-start(f32[2,17,2,512]{3,1,2,0:T(8,128)S(1)} %pad_maximum_fusion.1), channel_id=1, source_target_pairs={{16,0},{24,8},{32,16},{40,24},{48,32},{56,40},{64,48},{72,56},{80,... | collective-permute-start | bytes 417800 | tf_op jit(solution)/shard_map/ppermute | solution.py:16
  570.1 32.3 %collective-permute-start.18 = (f32[2,17,2,512]{3,1,2,0:T(8,128)S(1)}, f32[2,17,2,512]{3,1,2,0:T(8,128)S(1)}, u32[]{:S(2)}, u32[]{:S(2)}) collective-permute-start(f32[2,17,2,512]{3,1,2,0:T(8,128)S(1)} %pad_maximum_fusion.1), channel_id=1, source_target_pairs={{0,16},{8,24},{16,32},{24,40},{32,48},{40,56},{48,64},{56,72},{64,... | collective-permute-start | bytes 417800 | tf_op jit(solution)/shard_map/ppermute | solution.py:16
  592.7 10.6 %collective-permute-start.17 = (f32[2,17,2,512]{3,1,2,0:T(8,128)S(1)}, f32[2,17,2,512]{3,1,2,0:T(8,128)S(1)}, u32[]{:S(2)}, u32[]{:S(2)}) collective-permute-start(f32[2,17,2,512]{3,1,2,0:T(8,128)S(1)} %pad_maximum_fusion.1), channel_id=1, source_target_pairs={{8,0},{16,8},{24,16},{32,24},{40,32},{48,40},{56,48},{64,56},{72,6... | collective-permute-start | bytes 417800 | tf_op jit(solution)/shard_map/ppermute | solution.py:16
  595.8 14.5 %collective-permute-start.16 = (f32[2,17,2,512]{3,1,2,0:T(8,128)S(1)}, f32[2,17,2,512]{3,1,2,0:T(8,128)S(1)}, u32[]{:S(2)}, u32[]{:S(2)}) collective-permute-start(f32[2,17,2,512]{3,1,2,0:T(8,128)S(1)} %pad_maximum_fusion.1), channel_id=1, source_target_pairs={{0,8},{8,16},{16,24},{24,32},{32,40},{40,48},{48,56},{56,64},{64,7... | collective-permute-start | bytes 417800 | tf_op jit(solution)/shard_map/ppermute | solution.py:16
Sparse Core Ops, SparseCore 0:
  158.4 77.9 all-reduce.3
  314.6 72.5 all-reduce.5
  465.6 72.5 all-reduce.7
where the time goes:
time: 630 us; the launch traced here: 623 us
  waiting for transfers between devices  250 us (40%)
  starting transfers between devices  186 us (30%)
  other arithmetic  76 us (12%)
  local copies, waits for them, and re-layouts  56.4 us (9%)
  matrix products  20.2 us (3%)
  between operations  16.9 us (3%)
  blocking collectives  16.5 us (3%)
    psum x3, waiting for transfers between devices, local(): totals = lax.psum(partial_sums, 'bl')  223 us
    ppermute x24, starting transfers between devices, shifted(): return lax.ppermute(shard, axis, pairs)  173 us
    reduce_sum x7, other arithmetic, add_block(): real_part = jnp.sum(weights * jnp.cos(phases), axis=0)  57.6 us
    ppermute x24, waiting for transfers between devices, shifted(): return lax.ppermute(shard, axis, pairs)  18 us
    unnamed x15, local copies, waits for them, and re-layouts  17.3 us
    all_gather x1, blocking collectives, local(): lax.all_gather(baseline_wavelength_coords, 'bl', axis=2, tiled=True)  16.5 us
    dot_general x27, matrix products, weigh_piece(): jnp.dot(matrix, flattened, precision=lax.Precision.HIGHEST)  16.2 us
    all_to_all x1, starting transfers between devices, local(): lax.all_to_all(owned_model, 'bl', split_axis=4, concat_axis=1, tiled=True)  12.9 us
  transfers between devices with their start and end apart: 28, of which 7 were waited for; matrix products, arithmetic and copies ran while one was open for 4% of the time, Pallas kernels for 0%

commit v1 on v0

v1 whole, which is shorter than its diff:
```python
import jax
import jax.numpy as jnp
from jax import lax
from jax.experimental import pallas as pl
from jax.experimental.pallas import tpu as pltpu
from jax.sharding import PartitionSpec as P

F32 = jnp.float32
BF16 = jnp.bfloat16
MESH = pl.DeviceIdType.MESH
VMEM = pltpu.MemorySpace.VMEM
SMEM = pltpu.MemorySpace.SMEM

BL = 8
LINE = 4
RING = 16
ITERS = 3
DIRS = 16
TIMES = 16
STATIONS = 512
LANES = 128
REACH = 8.0
SPREAD = 4.0

SIN_HALF = (3.1415820213, -5.1671427567, 2.5418986016, -0.5546349618)
COS_HALF = (0.9999932956, -4.9339380202, 4.0412837185, -1.2221263189)


def horner(coefficients, at):
    value = coefficients[-1] * at + coefficients[-2]
    for coefficient in coefficients[-3::-1]:
        value = value * at + coefficient
    return value


def split_two(value):
    high = value.astype(BF16)
    low = (value - high.astype(F32)).astype(BF16)
    return high, low


def ratio_of(channel):
    return 0.5 + (channel.astype(F32) + 0.5) / 128.0


def gather_kernel(position, flux, spectral, count, pair, out, send, recv):
    me = lax.axis_index("bl")
    barrier = pltpu.get_barrier_semaphore()
    for step in range(1, BL):
        pl.semaphore_signal(barrier, inc=1, device_id={"bl": lax.rem(me + step, BL)}, device_id_type=MESH)
    first = lax.axis_index("freq") * 2

    def both(values):
        return jnp.concatenate([values[0:1], values[1:2]], axis=1)

    l = both(position[:, 0, :])
    m = both(position[:, 1, :])
    square = l * l + m * m
    n = -square / (1.0 + jnp.sqrt(1.0 - square))
    fluxes = both(flux[...])
    index = both(spectral[...])
    lane = lax.broadcasted_iota(jnp.int32, (1, LANES), 1)
    out[me, 0:1, :] = l
    out[me, 1:2, :] = m
    out[me, 2:3, :] = n
    extra = jnp.where(lane == 0, count[0].astype(F32), count[1].astype(F32))
    for channel in range(2):
        ratio = jnp.full((1, LANES), 1.0, F32) * ratio_of(first + channel)
        out[me, 3 + channel:4 + channel, :] = fluxes * jnp.exp(index * jnp.log(ratio))
        extra = jnp.where(lane == 2 + channel, ratio, extra)
    out[me, 5:6, :] = extra
    out[me, 6:8, :] = pair[...].astype(F32)

    pl.semaphore_wait(barrier, BL - 1)
    copies = []
    for step in range(1, BL):
        copy = pltpu.make_async_remote_copy(
            src_ref=out.at[me], dst_ref=out.at[me], send_sem=send.at[step], recv_sem=recv.at[step],
            device_id={"bl": lax.rem(me + step, BL)}, device_id_type=MESH)
        copy.start()
        copies.append(copy)
    for copy in copies:
        copy.wait()


def predict_kernel(params, coords, model):
    ratios = [params[5, 2], params[5, 3]]
    unroll = 4

    def one_patch(patch, _):
        row = (patch // 2) * 8
        column = (patch % 2) * 64
        live = params[row + 5, patch % 2].astype(jnp.int32)

        def some(turn, sums):
            sums = list(sums)
            for part in range(unroll):
                slot = turn * unroll + part
                at = column + slot
                l, m, n = params[row, at], params[row + 1, at], params[row + 2, at]
                delay = coords[0] * l + coords[1] * m + coords[2] * n
                for channel in range(2):
                    weight = jnp.where(slot < live, params[row + 3 + channel, at], 0.0)
                    turns = delay * ratios[channel]
                    turns = turns - jnp.round(turns)
                    square = turns * turns
                    sine = turns * horner(SIN_HALF, square)
                    cosine = horner(COS_HALF, square)
                    scaled = sine * weight
                    sums[3 * channel] += scaled * sine
                    sums[3 * channel + 1] += scaled * cosine
                    sums[3 * channel + 2] += weight
            return tuple(sums)

        zero = jnp.zeros((TIMES, LANES), F32)
        sums = lax.fori_loop(0, (live + unroll - 1) // unroll, some, (zero, zero, F32(0.0)) * 2)
        for channel in range(2):
            model[channel, patch, 0] = sums[3 * channel + 2] - 2.0 * sums[3 * channel]
            model[channel, patch, 1] = -2.0 * sums[3 * channel + 1]
        return 0

    lax.fori_loop(0, DIRS, one_patch, 0)


def calibrate_kernel(noise, model, params, true_gains, start_gains, flags,
                     gains_out, residual_out,
                     onehot, observed, joint_true, firsts, seconds, owned, first_out, first_in,
                     energy, energy_in, fits, fits_in, joint_out, joint_in, mixed, stage,
                     s_first, r_first, s_energy, r_energy, s_fit, r_fit, s_joint, r_joint,
                     s_mix, r_mix, s_gain, r_gain):
    freq = lax.axis_index("freq")
    bl = lax.axis_index("bl")
    y = lax.div(freq, 8)
    z_hi = lax.rem(lax.div(freq, LINE), 2)
    x = lax.rem(freq, LINE)
    me = z_hi * BL + bl
    above, below = y < lax.axis_size("freq") // 8 - 1, y > 0

    def ring(step):
        other = lax.rem(me + step, RING)
        device = {"freq": (y * 2 + lax.div(other, BL)) * LINE + x, "bl": lax.rem(other, BL)}
        return other, device

    def plane(other_y, other_x):
        return {"freq": (other_y * 2 + z_hi) * LINE + other_x, "bl": bl}

    mixed[...] = jnp.zeros(mixed.shape, F32)

    barrier = pltpu.get_barrier_semaphore()
    for step in range(1, RING):
        pl.semaphore_signal(barrier, inc=1, device_id=ring(step)[1], device_id_type=MESH)
    for step in range(1, LINE):
        pl.semaphore_signal(barrier, inc=1, device_id=plane(y, lax.rem(x + step, LINE)), device_id_type=MESH)

    @pl.when(above)
    def _():
        for other_x in range(LINE):
            pl.semaphore_signal(barrier, inc=1, device_id=plane(y + 1, other_x), device_id_type=MESH)

    @pl.when(below)
    def _():
        for other_x in range(LINE):
            pl.semaphore_signal(barrier, inc=1, device_id=plane(y - 1, other_x), device_id_type=MESH)

    station = lax.broadcasted_iota(jnp.int32, (STATIONS, LANES), 0).astype(F32)
    for source in range(BL):
        for end in range(2):
            ids = params[source * 8 + 6 + end:source * 8 + 7 + end, :]
            start = (source * 2 + end) * LANES
            onehot[:, start:start + LANES] = jnp.where(station == ids, 1.0, 0.0).astype(BF16)

    def local_joint(gains):
        own_onehot = onehot[:, pl.ds(pl.multiple_of(bl * 2 * LANES, 2 * LANES), 2 * LANES)]
        rows = []
        for part in range(2):
            rows.append(jnp.concatenate(
                [gains[pl.ds(tile * 2 + part, 32, stride=8), :] for tile in range(4)], axis=1))
        high, low = split_two(jnp.concatenate(rows, axis=0))
        ends = jnp.dot(jnp.concatenate([high, low], axis=0), own_onehot, preferred_element_type=F32)
        ends = ends[0:64] + ends[64:128]
        pr, pi = ends[0:32, 0:LANES], ends[32:64, 0:LANES]
        qr, qi = ends[0:32, LANES:], ends[32:64, LANES:]
        return pr * qr + pi * qi, pi * qr - pr * qi

    for ref, gains in ((joint_true, true_gains), (joint_in.at[0], start_gains)):
        parts = local_joint(gains)
        for channel in range(2):
            for part in range(2):
                for patch in range(DIRS):
                    at = channel * DIRS + patch
                    ref[patch, part * 2 + channel:part * 2 + channel + 1, :] = parts[part][at:at + 1]

    def corrupted(joint, channel):
        def add(patch, totals):
            jr = joint[patch, channel:channel + 1, :]
            ji = joint[patch, 2 + channel:3 + channel, :]
            mr, mi = model[channel, patch, 0], model[channel, patch, 1]
            return totals[0] + (jr * mr - ji * mi), totals[1] + (jr * mi + ji * mr)

        zero = jnp.zeros((TIMES, LANES), F32)
        return lax.fori_loop(0, DIRS, add, (zero, zero), unroll=True)

    for channel in range(2):
        totals = corrupted(joint_true, channel)
        for part in range(2):
            observed[channel, part] = noise[pl.ds(channel * 32 + part, TIMES, stride=2), :] + totals[part]

    def put_energy(patch, _):
        for channel in range(2):
            mr, mi = model[channel, patch, 0], model[channel, patch, 1]
            row = jnp.sum(mr * mr + mi * mi, axis=0, keepdims=True)
            weight = jnp.full((1, LANES), 1.0, F32) * (1.0 - flags[channel].astype(F32))
            for part in range(2):
                at = part * 2 + channel
                energy[patch, at:at + 1, :] = row
                energy[patch, 4 + at:5 + at, :] = weight
        return 0

    lax.fori_loop(0, DIRS, put_energy, 0, unroll=True)

    away = (1 - z_hi) * BL + bl
    for channel in range(2):
        first_out[channel] = start_gains[pl.ds(pl.multiple_of(channel * 128 + away * 8, 8), 8), :]

    neighbours = jnp.where(above, LINE, 0) + jnp.where(below, LINE, 0)
    pl.semaphore_wait(barrier, RING - 1 + LINE - 1 + neighbours)

    sends = []

    def remote(src, dst, send, recv, device):
        return pltpu.make_async_remote_copy(
            src_ref=src, dst_ref=dst, send_sem=send, recv_sem=recv, device_id=device, device_id_type=MESH)

    def to_ring(outgoing, incoming, send, recv):
        copies = []
        for step in range(1, RING):
            other, device = ring(step)
            copy = remote(outgoing.at[other], incoming.at[me], send.at[step], recv.at[step], device)
            copy.start()
            copies.append(copy)
        incoming[me] = outgoing[me]
        sends.extend(copies)
        return copies

    first_copy = remote(first_out, first_in, s_first, r_first, ring(BL)[1])
    first_copy.start()
    sends.append(first_copy)
    energy_copies = to_ring(energy, energy_in, s_energy, r_energy)

    row8 = lax.broadcasted_iota(jnp.int32, (8, LANES), 0)
    is_real = (row8 & 2) == 0

    def from_later(value):
        return pltpu.roll(value, 6, 0)

    def from_earlier(value):
        return pltpu.roll(value, 2, 0)

    def swapped(value):
        return jnp.where(is_real, from_later(value), from_earlier(value))

    def put_ends(gains):
        rows = jnp.concatenate([
            jnp.concatenate([gains[0:4], gains[8:12]], axis=0),
            jnp.concatenate([gains[4:8], gains[12:16]], axis=0)], axis=1)
        high, low = split_two(rows)
        both = jnp.dot(jnp.concatenate([high, low], axis=0), onehot[...], preferred_element_type=F32)
        both = both[0:8] + both[8:16]
        for source in range(BL):
            firsts[source] = both[:, source * 256:source * 256 + LANES]
            seconds[source] = both[:, source * 256 + LANES:source * 256 + 256]

    def to_halves(rows):
        return jnp.concatenate([
            rows[0:4, 0:256], rows[0:4, 256:512], rows[4:8, 0:256], rows[4:8, 256:512]], axis=0)

    here = lax.broadcasted_iota(jnp.int32, (16, 128), 0)
    there = lax.broadcasted_iota(jnp.int32, (16, 128), 1)
    slot = there >> 3
    slot_y = jnp.where(slot < 8, 0, jnp.where(slot < 12, 1, -1))
    slot_z = jnp.where(slot < 8, slot & 1, jnp.where(slot < 12, 1, 0))
    slot_x = jnp.where(slot < 8, slot >> 1, slot & 3)
    apart = (16 * slot_y + 8 * ((here >> 3) - slot_z) + 2 * (x - slot_x) + (here & 1) - (there & 1)).astype(F32)
    reached = jnp.where((here & 6) == (there & 6), jnp.where(jnp.abs(apart) <= REACH, 1.0, 0.0), 0.0)
    smoothing = jnp.exp(-(apart * apart) / (2.0 * SPREAD * SPREAD)) * reached

    def fitted(round_index):
        joint = joint_in.at[round_index]
        for channel in range(2):
            totals = corrupted(joint, channel)
            rest_r = observed[channel, 0] - totals[0]
            rest_i = observed[channel, 1] - totals[1]

            def put_fit(patch, _):
                mr, mi = model[channel, patch, 0], model[channel, patch, 1]
                power = energy[patch, channel:channel + 1, :]
                for part, value in enumerate((mr * rest_r + mi * rest_i, mr * rest_i - mi * rest_r)):
                    at = part * 2 + channel
                    row = jnp.sum(value, axis=0, keepdims=True)
                    fits[round_index, patch, at:at + 1, :] = row + joint[patch, at:at + 1, :] * power
                return 0

            lax.fori_loop(0, DIRS, put_fit, 0, unroll=True)

    inverse = None
    weight_halves = None
    weight_rows = None
    power_rows = []
    for turn in range(ITERS):
        if turn > 0:
            for copy in joint_copies:
                copy.wait_recv()
        fitted(turn)
        fit_copies = to_ring(fits.at[turn], fits_in.at[turn], s_fit.at[turn], r_fit.at[turn])
        if turn == 0:
            first_copy.wait_recv()
            for channel in range(2):
                own = start_gains[pl.ds(pl.multiple_of(channel * 128 + me * 8, 8), 8), :]
                other = first_in[channel]
                for row in range(8):
                    half, lane, part = row // 4, (row // 2) % 2, row % 2
                    at = half * 4 + part * 2 + channel
                    owned[z_hi, at:at + 1, lane * LANES:(lane + 1) * LANES] = own[row:row + 1]
                    owned[1 - z_hi, at:at + 1, lane * LANES:(lane + 1) * LANES] = other[row:row + 1]
            gains_now = owned[...].reshape(16, 256)
            put_ends(gains_now)
            for copy in energy_copies:
                copy.wait_recv()
            for source in range(BL):
                power_rows.append(jnp.concatenate([energy_in[source, 0:4], energy_in[BL + source, 0:4]], axis=0))
            weight_rows = jnp.concatenate([energy_in[0, 4:8], energy_in[BL, 4:8]], axis=0)
            weight_rows = jnp.concatenate([weight_rows] * 4, axis=1)
            weight_halves = to_halves(weight_rows)
        for copy in fit_copies:
            copy.wait_recv()

        columns = []
        for source in range(BL):
            fit = jnp.concatenate([fits_in[turn, source], fits_in[turn, BL + source]], axis=0)
            power = power_rows[source]
            for toward_first in (True, False):
                far = (seconds if toward_first else firsts)[source]
                far_swapped = swapped(far)
                direct = far * fit
                crossed = far_swapped * fit
                if toward_first:
                    numer = jnp.where(is_real, direct - from_later(direct), crossed + from_earlier(crossed))
                else:
                    numer = jnp.where(is_real, direct + from_later(direct), from_earlier(crossed) - crossed)
                denom = (far * far + far_swapped * far_swapped) * power
                high, low = split_two(jnp.concatenate([numer, denom], axis=0))
                columns.append(jnp.concatenate([high, low], axis=0))
        received = lax.dot_general(
            jnp.concatenate(columns, axis=1), onehot[...], (((1,), (1,)), ((), ())), preferred_element_type=F32)
        received = received[0:16] + received[16:32]
        solved = (received[0:8] * weight_rows) / jnp.maximum(received[8:16] * weight_rows, 1.0)
        blended = 0.5 * gains_now + 0.5 * to_halves(solved)
        packed = weight_halves * blended

        width = 384 if turn == 0 else 256
        for z in range(2):
            mixed[turn, 2 * x + z, :, 0:256] = packed[z * 8:z * 8 + 8]
            if turn == 0:
                mixed[turn, 2 * x + z, :, 256:384] = weight_halves[z * 8:z * 8 + 8, 0:LANES]

        def planes(first, count):
            return mixed.at[turn, pl.ds(first, count), :, pl.ds(0, width)]

        line_copies, far_copies = [], []
        for other_x in range(LINE):
            up = remote(planes(2 * x + 1, 1), planes(8 + x, 1), s_mix.at[turn, 3 + other_x],
                        r_mix.at[turn, 4 + x], plane(y + 1, other_x))
            down = remote(planes(2 * x, 1), planes(12 + x, 1), s_mix.at[turn, 7 + other_x],
                          r_mix.at[turn, 8 + x], plane(y - 1, other_x))
            far_copies.append((jnp.logical_and(above, other_x <= x), up))
            far_copies.append((jnp.logical_and(below, other_x >= x), down))
        for step in range(1, LINE):
            copy = remote(planes(2 * x, 2), planes(2 * x, 2), s_mix.at[turn, step - 1], r_mix.at[turn, x],
                          plane(y, lax.rem(x + step, LINE)))
            copy.start()
            line_copies.append(copy)
        for needed, copy in far_copies:
            pl.when(needed)(copy.start)

        for step in range(1, LINE):
            source_x = lax.rem(x + step, LINE)
            remote(planes(2 * source_x, 2), planes(2 * source_x, 2), s_mix.at[turn, step - 1],
                   r_mix.at[turn, source_x], plane(y, source_x)).wait_recv()
        for source_x in range(LINE):
            from_above = remote(planes(12 + source_x, 1), planes(12 + source_x, 1), s_mix.at[turn, 3 + source_x],
                                r_mix.at[turn, 8 + source_x], plane(y + 1, source_x))
            from_below = remote(planes(8 + source_x, 1), planes(8 + source_x, 1), s_mix.at[turn, 7 + source_x],
                                r_mix.at[turn, 4 + source_x], plane(y - 1, source_x))
            pl.when(jnp.logical_and(above, source_x <= x))(from_above.wait_recv)
            pl.when(jnp.logical_and(below, source_x >= x))(from_below.wait_recv)
        summed = jnp.dot(smoothing, mixed[turn, :, :, 0:width].reshape(128, width),
                         precision=lax.Precision.HIGHEST, preferred_element_type=F32)
        if turn == 0:
            inverse = 1.0 / jnp.maximum(summed[:, 256:384], 1.0)
            inverse = jnp.concatenate([inverse, inverse], axis=1)
        gains_now = summed[:, 0:256] * inverse

        put_ends(gains_now)
        for source in range(BL):
            near, far = firsts[source], seconds[source]
            direct = near * far
            crossed = near * swapped(far)
            joint = jnp.where(is_real, direct + from_later(direct), crossed - from_earlier(crossed))
            joint_out[turn, source] = joint[0:4]
            joint_out[turn, BL + source] = joint[4:8]
        joint_copies = to_ring(joint_out.at[turn], joint_in.at[turn + 1], s_joint.at[turn], r_joint.at[turn])

        for copy in line_copies:
            copy.wait_send()
        for needed, copy in far_copies:
            pl.when(needed)(copy.wait_send)

    for z in range(2):
        for channel in range(2):
            for row in range(8):
                half, lane, part = row // 4, (row // 2) % 2, row % 2
                at = z * 8 + half * 4 + part * 2 + channel
                stage[z, channel, row:row + 1, :] = gains_now[at:at + 1, lane * LANES:(lane + 1) * LANES]
    gain_copies = []
    for step in range(1, RING):
        other, device = ring(step)
        copy = remote(stage.at[lax.div(other, BL)], gains_out.at[:, me], s_gain.at[step], r_gain.at[step], device)
        copy.start()
        gain_copies.append(copy)
    sends.extend(gain_copies)
    gains_out[:, me] = stage[z_hi]

    for copy in joint_copies:
        copy.wait_recv()
    for channel in range(2):
        totals = corrupted(joint_in.at[ITERS], channel)
        for part in range(2):
            residual_out[pl.ds(channel * 32 + part, TIMES, stride=2), :] = observed[channel, part] - totals[part]
    for copy in gain_copies:
        copy.wait_recv()
    for copy in sends:
        copy.wait_send()


def local(visibility_noise, baseline_wavelength_coords, station_pair, comp_position, comp_flux,
          comp_spectral, comp_count, true_gains, start_gains, channel_flags):
    vmem = pl.BlockSpec(memory_space=VMEM)
    smem = pl.BlockSpec(memory_space=SMEM)
    dma = pltpu.SemaphoreType.DMA
    params = pl.pallas_call(
        gather_kernel,
        out_shape=jax.ShapeDtypeStruct((BL, 8, LANES), F32),
        in_specs=[vmem, vmem, vmem, smem, vmem],
        out_specs=vmem,
        scratch_shapes=[dma((BL,)), dma((BL,))],
        compiler_params=pltpu.CompilerParams(collective_id=0, has_side_effects=True),
        name="gather_params",
    )(comp_position, comp_flux, comp_spectral, comp_count, station_pair)
    params = params.reshape(BL * 8, LANES)
    model = pl.pallas_call(
        predict_kernel,
        out_shape=jax.ShapeDtypeStruct((2, DIRS, 2, TIMES, LANES), F32),
        in_specs=[smem, vmem],
        out_specs=vmem,
        name="predict",
    )(params, baseline_wavelength_coords)

    def tiles(gains):
        return gains.reshape(2, DIRS, 2, 4, LANES).transpose(0, 1, 3, 2, 4).reshape(2 * DIRS * 8, LANES)

    gains, residual = pl.pallas_call(
        calibrate_kernel,
        out_shape=(jax.ShapeDtypeStruct((2, DIRS, 8, LANES), F32), jax.ShapeDtypeStruct((64, LANES), F32)),
        in_specs=[vmem, vmem, vmem, vmem, vmem, smem],
        out_specs=(vmem, vmem),
        scratch_shapes=[
            pltpu.VMEM((STATIONS, BL * 2 * LANES), BF16),
            pltpu.VMEM((2, 2, TIMES, LANES), F32),
            pltpu.VMEM((DIRS, 4, LANES), F32),
            pltpu.VMEM((BL, 8, LANES), F32),
            pltpu.VMEM((BL, 8, LANES), F32),
            pltpu.VMEM((2, 8, 256), F32),
            pltpu.VMEM((2, 8, LANES), F32),
            pltpu.VMEM((2, 8, LANES), F32),
            pltpu.VMEM((RING, 8, LANES), F32),
            pltpu.VMEM((RING, 8, LANES), F32),
            pltpu.VMEM((ITERS, RING, 4, LANES), F32),
            pltpu.VMEM((ITERS, RING, 4, LANES), F32),
            pltpu.VMEM((ITERS, RING, 4, LANES), F32),
            pltpu.VMEM((ITERS + 1, RING, 4, LANES), F32),
            pltpu.VMEM((ITERS, 16, 8, 384), F32),
            pltpu.VMEM((2, 2, 8, LANES), F32),
            dma(()), dma(()),
            dma((RING,)), dma((RING,)),
            dma((ITERS, RING)), dma((ITERS, RING)),
            dma((ITERS, RING)), dma((ITERS, RING)),
            dma((ITERS, 11)), dma((ITERS, 12)),
            dma((RING,)), dma((RING,)),
        ],
        compiler_params=pltpu.CompilerParams(
            collective_id=1, has_side_effects=True, vmem_limit_bytes=32 * 1024 * 1024),
        name="calibrate",
    )(visibility_noise.reshape(64, LANES), model, params, tiles(true_gains), tiles(start_gains), channel_flags)
    gains = gains.reshape(2, DIRS, 4, 2, LANES).transpose(0, 1, 3, 2, 4).reshape(2, DIRS, 2, STATIONS)
    return gains, residual.reshape(2, TIMES, 2, LANES)


def solution(mesh):
    in_specs = (
        P("freq", None, None, "bl"),
        P(None, None, "bl"),
        P(None, "bl"),
        P("bl", None, None),
        P("bl", None),
        P("bl", None),
        P("bl"),
        P("freq", None, None, None),
        P("freq", None, None, None),
        P("freq"),
    )
    out_specs = (P("freq", None, None, None), P("freq", None, None, "bl"))
    return jax.shard_map(local, mesh=mesh, in_specs=in_specs, out_specs=out_specs, check_vma=False)
```

time: 630 us -> 87.5 us (0.14)
  the two profiles are of different devices: /device:TPU:24 before, /device:TPU:31 now
where the time goes in v1:
time: 87.5 us; the launch traced here: 87.2 us
  Pallas kernels  84.1 us (96%)
  local copies, waits for them, and re-layouts  2.34 us (3%)
    pallas_call x1, Pallas kernels, local(): pl.pallas_call(calibrate_kernel, out_shape=(jax.ShapeDtypeStruct((2, DIRS...  61.8 us
    pallas_call x1, Pallas kernels, local(): pl.pallas_call(predict_kernel, out_shape=jax.ShapeDtypeStruct((2, DIRS, 2...  11.5 us
    pallas_call x1, Pallas kernels, local(): pl.pallas_call(gather_kernel, out_shape=jax.ShapeDtypeStruct((BL, 8, LANE...  10.8 us
    unnamed x14, local copies, waits for them, and re-layouts  2.34 us

profile of v1, /device:TPU:31, one launch (start us, length us, event | category | flops | bytes accessed | tf_op | source)
XLA Modules:
  0.0 87.2 jit_solution(10067528398863320907)
XLA Ops:
  0.6 10.8 %gather_params.1 = f32[8,8,128]{2,1,0:T(8,128)} custom-call(f32[2,2,64]{2,1,0:T(2,128)} %position.1, f32[2,64]{1,0:T(2,128)} %flux.1, f32[2,64]{1,0:T(2,128)} %spectral.1, s32[2]{0:T(128)} %count.1, s32[2,128]{1,0:T(2,128)} %pair.1), custom_call_target="tpu_custom_call" | custom-call | tf_op jit(solution)/shard_map/gather_params/pallas_call | solution.py:450
  11.4 0.0 copy-start.1
  11.4 0.0 copy-start.2
  11.5 0.0 copy-start.3
  11.5 0.0 copy-start.4
  11.5 0.0 copy-start.5
  11.5 11.5 %predict.1.model = f32[2,16,2,16,128]{4,3,2,1,0:T(8,128)} custom-call(f32[64,128]{1,0:T(8,128)} %bitcast.18, f32[3,16,128]{2,1,0:T(8,128)} %coords.1), custom_call_target="tpu_custom_call" | custom-call | tf_op jit(solution)/shard_map/predict/pallas_call | solution.py:460
  23.0 0.0 copy-done.1
  23.0 0.0 copy-done.2
  23.0 0.0 copy-done.3
  23.0 0.0 copy-done.4
  23.0 0.0 copy-done.5
  23.0 0.0 copy-start
  23.0 1.0 %copy-done = f32[2,16,2,16,128]{4,3,2,1,0:T(8,128)S(1)} copy-done((f32[2,16,2,16,128]{4,3,2,1,0:T(8,128)S(1)}, f32[2,16,2,16,128]{4,3,2,1,0:T(8,128)}, u32[]{:S(2)}) %copy-start) | copy-done | bytes 524312
  24.1 61.8 %calibrate.1 = (f32[2,16,8,128]{3,2,1,0:T(8,128)S(1)}, f32[64,128]{1,0:T(8,128)S(1)}) custom-call(f32[64,128]{1,0:T(8,128)S(1)} %bitcast.23, f32[2,16,2,16,128]{4,3,2,1,0:T(8,128)S(1)} %copy-done, f32[64,128]{1,0:T(8,128)S(1)} %bitcast.19, f32[256,128]{1,0:T(8,128)S(1)} %bitcast.21, f32[256,128]{1,0:T(8,128)S(1)} %bitcast.22, s32[2]{0:T(128)S(1)} %copy-done.5), custom_call_target="tpu_custom_call" | custom-call | tf_op jit(solution)/shard_map/calibrate/pallas_call | solution.py:471
  85.9 0.7 copy.17
  86.6 0.6 copy.18
Async XLA Ops:
  11.4 11.6 %copy-start.1 = (f32[8,8,128]{2,1,0:T(8,128)S(1)}, f32[8,8,128]{2,1,0:T(8,128)}, u32[]{:S(2)}) copy-start(f32[8,8,128]{2,1,0:T(8,128)} %gather_params.1) | copy-start | bytes 98308
  11.4 11.5 %copy-start.2 = (f32[2,16,2,512]{3,2,1,0:T(2,128)S(1)}, f32[2,16,2,512]{3,2,1,0:T(2,128)}, u32[]{:S(2)}) copy-start(f32[2,16,2,512]{3,2,1,0:T(2,128)} %param.17) | copy-start | bytes 393220
  11.5 11.5 %copy-start.3 = (f32[2,16,2,512]{3,2,1,0:T(2,128)S(1)}, f32[2,16,2,512]{3,2,1,0:T(2,128)}, u32[]{:S(2)}) copy-start(f32[2,16,2,512]{3,2,1,0:T(2,128)} %param.18) | copy-start | bytes 393220
  11.5 11.5 %copy-start.4 = (f32[2,16,2,128]{3,2,1,0:T(2,128)S(1)}, f32[2,16,2,128]{3,2,1,0:T(2,128)}, u32[]{:S(2)}) copy-start(f32[2,16,2,128]{3,2,1,0:T(2,128)} %param.10) | copy-start | bytes 98308
  11.5 11.5 %copy-start.5 = (s32[2]{0:T(128)S(1)}, s32[2]{0:T(128)}, u32[]{:S(2)}) copy-start(s32[2]{0:T(128)} %flags.1) | copy-start | bytes 28
  23.0 1.0 %copy-start = (f32[2,16,2,16,128]{4,3,2,1,0:T(8,128)S(1)}, f32[2,16,2,16,128]{4,3,2,1,0:T(8,128)}, u32[]{:S(2)}) copy-start(f32[2,16,2,16,128]{4,3,2,1,0:T(8,128)} %predict.1.model) | copy-start | bytes 1572868

commit v2 on v1

--- a/solution.py
+++ b/solution.py
@@ -18,19 +18,17 @@
 DIRS = 16
 TIMES = 16
 STATIONS = 512
+COMPONENTS = 512
 LANES = 128
 REACH = 8.0
 SPREAD = 4.0
 
-SIN_HALF = (3.1415820213, -5.1671427567, 2.5418986016, -0.5546349618)
-COS_HALF = (0.9999932956, -4.9339380202, 4.0412837185, -1.2221263189)
-
-
-def horner(coefficients, at):
-    value = coefficients[-1] * at + coefficients[-2]
-    for coefficient in coefficients[-3::-1]:
-        value = value * at + coefficient
-    return value
+SIN_SCALE, SIN_FACTORS = -0.5546349618, (-0.978320908350836, -3.6046909402902565, 5.789750187942454)
+COS_SCALE, COS_FACTORS = -1.2221263189, (-0.24999786765951873, -3.0567664626737323, 3.2729900649797434)
+
+
+def factored(factors, at):
+    return (at + factors[0]) * (at * (at + factors[1]) + factors[2])
 
 
 def split_two(value):
@@ -43,89 +41,12 @@
     return 0.5 + (channel.astype(F32) + 0.5) / 128.0
 
 
-def gather_kernel(position, flux, spectral, count, pair, out, send, recv):
-    me = lax.axis_index("bl")
-    barrier = pltpu.get_barrier_semaphore()
-    for step in range(1, BL):
-        pl.semaphore_signal(barrier, inc=1, device_id={"bl": lax.rem(me + step, BL)}, device_id_type=MESH)
-    first = lax.axis_index("freq") * 2
-
-    def both(values):
-        return jnp.concatenate([values[0:1], values[1:2]], axis=1)
-
-    l = both(position[:, 0, :])
-    m = both(position[:, 1, :])
-    square = l * l + m * m
-    n = -square / (1.0 + jnp.sqrt(1.0 - square))
-    fluxes = both(flux[...])
-    index = both(spectral[...])
-    lane = lax.broadcasted_iota(jnp.int32, (1, LANES), 1)
-    out[me, 0:1, :] = l
-    out[me, 1:2, :] = m
-    out[me, 2:3, :] = n
-    extra = jnp.where(lane == 0, count[0].astype(F32), count[1].astype(F32))
-    for channel in range(2):
-        ratio = jnp.full((1, LANES), 1.0, F32) * ratio_of(first + channel)
-        out[me, 3 + channel:4 + channel, :] = fluxes * jnp.exp(index * jnp.log(ratio))
-        extra = jnp.where(lane == 2 + channel, ratio, extra)
-    out[me, 5:6, :] = extra
-    out[me, 6:8, :] = pair[...].astype(F32)
-
-    pl.semaphore_wait(barrier, BL - 1)
-    copies = []
-    for step in range(1, BL):
-        copy = pltpu.make_async_remote_copy(
-            src_ref=out.at[me], dst_ref=out.at[me], send_sem=send.at[step], recv_sem=recv.at[step],
-            device_id={"bl": lax.rem(me + step, BL)}, device_id_type=MESH)
-        copy.start()
-        copies.append(copy)
-    for copy in copies:
-        copy.wait()
-
-
-def predict_kernel(params, coords, model):
-    ratios = [params[5, 2], params[5, 3]]
-    unroll = 4
-
-    def one_patch(patch, _):
-        row = (patch // 2) * 8
-        column = (patch % 2) * 64
-        live = params[row + 5, patch % 2].astype(jnp.int32)
-
-        def some(turn, sums):
-            sums = list(sums)
-            for part in range(unroll):
-                slot = turn * unroll + part
-                at = column + slot
-                l, m, n = params[row, at], params[row + 1, at], params[row + 2, at]
-                delay = coords[0] * l + coords[1] * m + coords[2] * n
-                for channel in range(2):
-                    weight = jnp.where(slot < live, params[row + 3 + channel, at], 0.0)
-                    turns = delay * ratios[channel]
-                    turns = turns - jnp.round(turns)
-                    square = turns * turns
-                    sine = turns * horner(SIN_HALF, square)
-                    cosine = horner(COS_HALF, square)
-                    scaled = sine * weight
-                    sums[3 * channel] += scaled * sine
-                    sums[3 * channel + 1] += scaled * cosine
-                    sums[3 * channel + 2] += weight
-            return tuple(sums)
-
-        zero = jnp.zeros((TIMES, LANES), F32)
-        sums = lax.fori_loop(0, (live + unroll - 1) // unroll, some, (zero, zero, F32(0.0)) * 2)
-        for channel in range(2):
-            model[channel, patch, 0] = sums[3 * channel + 2] - 2.0 * sums[3 * channel]
-            model[channel, patch, 1] = -2.0 * sums[3 * channel + 1]
-        return 0
-
-    lax.fori_loop(0, DIRS, one_patch, 0)
-
-
-def calibrate_kernel(noise, model, params, true_gains, start_gains, flags,
+def calibrate_kernel(noise_hbm, coords_hbm, pair, position, flux, spectral, count, true_hbm, start_hbm, flags,
                      gains_out, residual_out,
-                     onehot, observed, joint_true, firsts, seconds, owned, first_out, first_in,
+                     noise, coords, true_gains, start_gains, params, ids, params_scalar, ids_scalar, running, model,
+                     own_onehot, onehot, observed, joint_true, firsts, seconds, owned, first_out, first_in,
                      energy, energy_in, fits, fits_in, joint_out, joint_in, mixed, stage,
+                     s_load, s_param, r_param, s_ids, r_ids,
                      s_first, r_first, s_energy, r_energy, s_fit, r_fit, s_joint, r_joint,
                      s_mix, r_mix, s_gain, r_gain):
     freq = lax.axis_index("freq")
@@ -144,6 +65,13 @@
     def plane(other_y, other_x):
         return {"freq": (other_y * 2 + z_hi) * LINE + other_x, "bl": bl}
 
+    loads = []
+    for index, (source, target) in enumerate((
+            (true_hbm, true_gains), (start_hbm, start_gains), (noise_hbm, noise), (coords_hbm, coords))):
+        copy = pltpu.make_async_copy(source, target, s_load.at[index])
+        copy.start()
+        loads.append(copy)
+
     mixed[...] = jnp.zeros(mixed.shape, F32)
 
     barrier = pltpu.get_barrier_semaphore()
@@ -162,21 +90,43 @@
         for other_x in range(LINE):
             pl.semaphore_signal(barrier, inc=1, device_id=plane(y - 1, other_x), device_id_type=MESH)
 
-    station = lax.broadcasted_iota(jnp.int32, (STATIONS, LANES), 0).astype(F32)
-    for source in range(BL):
-        for end in range(2):
-            ids = params[source * 8 + 6 + end:source * 8 + 7 + end, :]
-            start = (source * 2 + end) * LANES
-            onehot[:, start:start + LANES] = jnp.where(station == ids, 1.0, 0.0).astype(BF16)
+    def both(values):
+        return jnp.concatenate([values[0:1], values[1:2]], axis=1)
+
+    l, m = both(position[:, 0, :]), both(position[:, 1, :])
+    square = l * l + m * m
+    params[bl, 0:1, :] = l
+    params[bl, 1:2, :] = m
+    params[bl, 2:3, :] = -square / (1.0 + jnp.sqrt(1.0 - square))
+    lane = lax.broadcasted_iota(jnp.int32, (1, LANES), 1)
+    lives = jnp.where(lane < 64, count[0], count[1])
+    fluxes = jnp.where((lane & 63) < lives, both(flux[...]), 0.0)
+    index = both(spectral[...])
+    extra = jnp.zeros((1, LANES), F32)
+    for channel in range(2):
+        ratio = jnp.full((1, LANES), 1.0, F32) * ratio_of(freq * 2 + channel)
+        spectrum = fluxes * jnp.exp(index * jnp.log(ratio))
+        params[bl, 3 + channel:4 + channel, :] = spectrum
+        for half in range(2):
+            total = jnp.sum(jnp.where((lane >> 6) == half, spectrum, 0.0), axis=1, keepdims=True)
+            extra = jnp.where(lane == half * 2 + channel, total, extra)
+    params[bl, 5:6, :] = extra
+    ids[bl, 0:2, :] = pair[...]
+    ids[bl, 2:3, :] = jnp.where(lane == 0, count[0], count[1])
+
+    station = lax.broadcasted_iota(jnp.int32, (STATIONS, LANES), 0)
+    for end in range(2):
+        own_onehot[:, end * LANES:(end + 1) * LANES] = jnp.where(station == pair[end:end + 1, :], 1.0, 0.0).astype(BF16)
+    for copy in loads:
+        copy.wait()
 
     def local_joint(gains):
-        own_onehot = onehot[:, pl.ds(pl.multiple_of(bl * 2 * LANES, 2 * LANES), 2 * LANES)]
         rows = []
         for part in range(2):
             rows.append(jnp.concatenate(
                 [gains[pl.ds(tile * 2 + part, 32, stride=8), :] for tile in range(4)], axis=1))
         high, low = split_two(jnp.concatenate(rows, axis=0))
-        ends = jnp.dot(jnp.concatenate([high, low], axis=0), own_onehot, preferred_element_type=F32)
+        ends = jnp.dot(jnp.concatenate([high, low], axis=0), own_onehot[...], preferred_element_type=F32)
         ends = ends[0:64] + ends[64:128]
         pr, pi = ends[0:32, 0:LANES], ends[32:64, 0:LANES]
         qr, qi = ends[0:32, LANES:], ends[32:64, LANES:]
@@ -189,6 +139,81 @@
                 for patch in range(DIRS):
                     at = channel * DIRS + patch
                     ref[patch, part * 2 + channel:part * 2 + channel + 1, :] = parts[part][at:at + 1]
+
+    away = (1 - z_hi) * BL + bl
+    for channel in range(2):
+        first_out[channel] = start_gains[pl.ds(pl.multiple_of(channel * 128 + away * 8, 8), 8), :]
+
+    neighbours = jnp.where(above, LINE, 0) + jnp.where(below, LINE, 0)
+    pl.semaphore_wait(barrier, RING - 1 + LINE - 1 + neighbours)
+
+    sends = []
+
+    def remote(src, dst, send, recv, device):
+        return pltpu.make_async_remote_copy(
+            src_ref=src, dst_ref=dst, send_sem=send, recv_sem=recv, device_id=device, device_id_type=MESH)
+
+    param_copies = []
+    for step in (4, 3, 5, 2, 6, 1, 7):
+        device = {"bl": lax.rem(bl + step, BL)}
+        for outgoing, send, recv in ((params, s_param, r_param), (ids, s_ids, r_ids)):
+            copy = remote(outgoing.at[bl], outgoing.at[bl], send.at[step], recv.at[step], device)
+            copy.start()
+            param_copies.append(copy)
+    sends.extend(param_copies)
+    first_copy = remote(first_out, first_in, s_first, r_first, ring(BL)[1])
+    first_copy.start()
+    sends.append(first_copy)
+    for copy in param_copies:
+        copy.wait_recv()
+    scalars = [pltpu.make_async_copy(params, params_scalar, s_load.at[4]),
+               pltpu.make_async_copy(ids, ids_scalar, s_load.at[5])]
+    for copy in scalars:
+        copy.start()
+    for copy in scalars:
+        copy.wait()
+
+    ratio_zero, ratio_one = ratio_of(freq * 2), ratio_of(freq * 2 + 1)
+    relative = ratio_one / ratio_zero
+    u, v, w = coords[0] * ratio_zero, coords[1] * ratio_zero, coords[2] * ratio_zero
+
+    def lives_of(patch):
+        return ids_scalar[patch >> 1, 2, patch & 1]
+
+    def one_component(component, state):
+        sums, (patch, slot, live) = list(state[0:4]), state[4:7]
+        device, column = patch >> 1, (patch & 1) * 64 + slot
+        delay = (u * params_scalar[device, 0, column] + v * params_scalar[device, 1, column]
+                 + w * params_scalar[device, 2, column])
+        keep = jnp.where(slot == 0, 0.0, 1.0)
+        for channel, turns in enumerate((delay, delay * relative)):
+            turns = turns - jnp.round(turns)
+            square = turns * turns
+            sine = turns * factored(SIN_FACTORS, square)
+            scaled = sine * params_scalar[device, 3 + channel, column]
+            sums[2 * channel] = sums[2 * channel] * keep + scaled * sine
+            sums[2 * channel + 1] = sums[2 * channel + 1] * keep + scaled * factored(COS_FACTORS, square)
+        for place in range(4):
+            running[component, place] = sums[place]
+        done = slot + 1 >= live
+        patch = jnp.minimum(patch + jnp.where(done, 1, 0), DIRS - 1)
+        slot = jnp.where(done, 0, slot + 1)
+        return (*sums, patch, slot, lives_of(patch))
+
+    zero = jnp.zeros((TIMES, LANES), F32)
+    start = jnp.int32(0)
+    lax.fori_loop(0, COMPONENTS, one_component, (zero,) * 4 + (start, start, lives_of(start)), unroll=16)
+
+    def finish_patch(patch, end):
+        end = end + lives_of(patch)
+        last = jnp.clip(end - 1, 0, COMPONENTS - 1)
+        for channel in range(2):
+            total = params_scalar[patch >> 1, 5, (patch & 1) * 2 + channel]
+            model[channel, patch, 0] = total - (2.0 * SIN_SCALE * SIN_SCALE) * running[last, 2 * channel]
+            model[channel, patch, 1] = (-2.0 * SIN_SCALE * COS_SCALE) * running[last, 2 * channel + 1]
+        return end
+
+    lax.fori_loop(0, DIRS, finish_patch, start, unroll=True)
 
     def corrupted(joint, channel):
         def add(patch, totals):
@@ -218,19 +243,6 @@
 
     lax.fori_loop(0, DIRS, put_energy, 0, unroll=True)
 
-    away = (1 - z_hi) * BL + bl
-    for channel in range(2):
-        first_out[channel] = start_gains[pl.ds(pl.multiple_of(channel * 128 + away * 8, 8), 8), :]
-
-    neighbours = jnp.where(above, LINE, 0) + jnp.where(below, LINE, 0)
-    pl.semaphore_wait(barrier, RING - 1 + LINE - 1 + neighbours)
-
-    sends = []
-
-    def remote(src, dst, send, recv, device):
-        return pltpu.make_async_remote_copy(
-            src_ref=src, dst_ref=dst, send_sem=send, recv_sem=recv, device_id=device, device_id_type=MESH)
-
     def to_ring(outgoing, incoming, send, recv):
         copies = []
         for step in range(1, RING):
@@ -242,9 +254,6 @@
         sends.extend(copies)
         return copies
 
-    first_copy = remote(first_out, first_in, s_first, r_first, ring(BL)[1])
-    first_copy.start()
-    sends.append(first_copy)
     energy_copies = to_ring(energy, energy_in, s_energy, r_energy)
 
     row8 = lax.broadcasted_iota(jnp.int32, (8, LANES), 0)
@@ -313,6 +322,11 @@
         fitted(turn)
         fit_copies = to_ring(fits.at[turn], fits_in.at[turn], s_fit.at[turn], r_fit.at[turn])
         if turn == 0:
+            for source in range(BL):
+                for end in range(2):
+                    row = ids[source, end:end + 1, :]
+                    start = (source * 2 + end) * LANES
+                    onehot[:, start:start + LANES] = jnp.where(station == row, 1.0, 0.0).astype(BF16)
             first_copy.wait_recv()
             for channel in range(2):
                 own = start_gains[pl.ds(pl.multiple_of(channel * 128 + me * 8, 8), 8), :]
@@ -446,34 +460,28 @@
           comp_spectral, comp_count, true_gains, start_gains, channel_flags):
     vmem = pl.BlockSpec(memory_space=VMEM)
     smem = pl.BlockSpec(memory_space=SMEM)
+    anywhere = pl.BlockSpec(memory_space=pltpu.MemorySpace.HBM)
     dma = pltpu.SemaphoreType.DMA
-    params = pl.pallas_call(
-        gather_kernel,
-        out_shape=jax.ShapeDtypeStruct((BL, 8, LANES), F32),
-        in_specs=[vmem, vmem, vmem, smem, vmem],
-        out_specs=vmem,
-        scratch_shapes=[dma((BL,)), dma((BL,))],
-        compiler_params=pltpu.CompilerParams(collective_id=0, has_side_effects=True),
-        name="gather_params",
-    )(comp_position, comp_flux, comp_spectral, comp_count, station_pair)
-    params = params.reshape(BL * 8, LANES)
-    model = pl.pallas_call(
-        predict_kernel,
-        out_shape=jax.ShapeDtypeStruct((2, DIRS, 2, TIMES, LANES), F32),
-        in_specs=[smem, vmem],
-        out_specs=vmem,
-        name="predict",
-    )(params, baseline_wavelength_coords)
-
     def tiles(gains):
         return gains.reshape(2, DIRS, 2, 4, LANES).transpose(0, 1, 3, 2, 4).reshape(2 * DIRS * 8, LANES)
 
     gains, residual = pl.pallas_call(
         calibrate_kernel,
         out_shape=(jax.ShapeDtypeStruct((2, DIRS, 8, LANES), F32), jax.ShapeDtypeStruct((64, LANES), F32)),
-        in_specs=[vmem, vmem, vmem, vmem, vmem, smem],
+        in_specs=[anywhere, anywhere, vmem, vmem, vmem, vmem, smem, anywhere, anywhere, smem],
         out_specs=(vmem, vmem),
         scratch_shapes=[
+            pltpu.VMEM((64, LANES), F32),
+            pltpu.VMEM((3, TIMES, LANES), F32),
+            pltpu.VMEM((256, LANES), F32),
+            pltpu.VMEM((256, LANES), F32),
+            pltpu.VMEM((BL, 8, LANES), F32),
+            pltpu.VMEM((BL, 8, LANES), jnp.int32),
+            pltpu.SMEM((BL, 8, LANES), F32),
+            pltpu.SMEM((BL, 8, LANES), jnp.int32),
+            pltpu.VMEM((COMPONENTS, 4, TIMES, LANES), F32),
+            pltpu.VMEM((2, DIRS, 2, TIMES, LANES), F32),
+            pltpu.VMEM((STATIONS, 2 * LANES), BF16),
             pltpu.VMEM((STATIONS, BL * 2 * LANES), BF16),
             pltpu.VMEM((2, 2, TIMES, LANES), F32),
             pltpu.VMEM((DIRS, 4, LANES), F32),
@@ -490,6 +498,7 @@
             pltpu.VMEM((ITERS + 1, RING, 4, LANES), F32),
             pltpu.VMEM((ITERS, 16, 8, 384), F32),
             pltpu.VMEM((2, 2, 8, LANES), F32),
+            dma((6,)), dma((BL,)), dma((BL,)), dma((BL,)), dma((BL,)),
             dma(()), dma(()),
             dma((RING,)), dma((RING,)),
             dma((ITERS, RING)), dma((ITERS, RING)),
@@ -498,9 +507,10 @@
             dma((RING,)), dma((RING,)),
         ],
         compiler_params=pltpu.CompilerParams(
-            collective_id=1, has_side_effects=True, vmem_limit_bytes=32 * 1024 * 1024),
+            collective_id=0, has_side_effects=True, vmem_limit_bytes=56 * 1024 * 1024),
         name="calibrate",
-    )(visibility_noise.reshape(64, LANES), model, params, tiles(true_gains), tiles(start_gains), channel_flags)
+    )(visibility_noise.reshape(64, LANES), baseline_wavelength_coords, station_pair, comp_position, comp_flux,
+      comp_spectral, comp_count, tiles(true_gains), tiles(start_gains), channel_flags)
     gains = gains.reshape(2, DIRS, 4, 2, LANES).transpose(0, 1, 3, 2, 4).reshape(2, DIRS, 2, STATIONS)
     return gains, residual.reshape(2, TIMES, 2, LANES)
 

time: 87.5 us -> 84.2 us (0.962)
  Pallas kernels: 84.1 us -> 81.2 us
    pallas_call x2 -> x0, Pallas kernels: 22.3 us -> none  [the longest x1 11.5 us: local(): pl.pallas_call(predict_kernel, out_shape=jax.ShapeDtypeStruct((2, DIRS, 2...]
    pallas_call x1, Pallas kernels: 61.8 us -> 81.2 us  [local(): pl.pallas_call(calibrate_kernel, out_shape=(jax.ShapeDtypeStruct((2, DIRS...]
    unnamed x14 -> x4, local copies, waits for them, and re-layouts: 2.34 us -> 2.19 us
where the time goes in v2:
time: 84.2 us; the launch traced here: 84.1 us
  Pallas kernels  81.2 us (96%)
  local copies, waits for them, and re-layouts  2.19 us (3%)
    pallas_call x1, Pallas kernels, local(): pl.pallas_call(calibrate_kernel, out_shape=(jax.ShapeDtypeStruct((2, DIRS...  81.2 us
    unnamed x4, local copies, waits for them, and re-layouts  2.19 us

profile of v2, /device:TPU:31, one launch (start us, length us, event | category | flops | bytes accessed | tf_op | source)
XLA Modules:
  0.0 84.1 jit_solution(4643462958978024691)
XLA Ops:
  0.6 81.2 %calibrate.1 = (f32[2,16,8,128]{3,2,1,0:T(8,128)}, f32[64,128]{1,0:T(8,128)}) custom-call(f32[64,128]{1,0:T(8,128)} %bitcast.20, f32[3,16,128]{2,1,0:T(8,128)} %coords_hbm.1, s32[2,128]{1,0:T(2,128)} %pair.1, f32[2,2,64]{2,1,0:T(2,128)} %position.1, f32[2,64]{1,0:T(2,128)} %flux.1, f32[2,64]{1,0:T(2,128)} %spectral.1, s32[2]{0:T(128)} %count.1, ...), custom_call_target="tpu_custom_call" | custom-call | tf_op jit(solution)/shard_map/calibrate/pallas_call | solution.py:468
  81.9 0.0 copy-start
  81.9 1.6 %copy.17 = f32[2,16,2,512]{3,2,1,0:T(2,128)} copy(f32[2,16,2,512]{3,2,1,0:T(2,128)} %bitcast.19) | data formatting | bytes 262144
  83.5 0.0 copy-done
  83.5 0.6 copy.18
Async XLA Ops:
  81.9 1.6 %copy-start = (f32[64,128]{1,0:T(8,128)S(1)}, f32[64,128]{1,0:T(8,128)}, u32[]{:S(2)}) copy-start(f32[64,128]{1,0:T(8,128)} %get-tuple-element.5) | copy-start | bytes 98308

commit v3 on v2

--- a/solution.py
+++ b/solution.py
@@ -11,6 +11,7 @@
 VMEM = pltpu.MemorySpace.VMEM
 SMEM = pltpu.MemorySpace.SMEM
 
+FAR_FIRST = (8, 7, 9, 6, 10, 5, 11, 4, 12, 3, 13, 2, 14, 1, 15)
 BL = 8
 LINE = 4
 RING = 16
@@ -245,7 +246,7 @@
 
     def to_ring(outgoing, incoming, send, recv):
         copies = []
-        for step in range(1, RING):
+        for step in FAR_FIRST:
             other, device = ring(step)
             copy = remote(outgoing.at[other], incoming.at[me], send.at[step], recv.at[step], device)
             copy.start()
@@ -310,6 +311,9 @@
                 return 0
 
             lax.fori_loop(0, DIRS, put_fit, 0, unroll=True)
+
+    smoothing_high, smoothing_low = split_two(smoothing)
+    smoothing_both = jnp.concatenate([smoothing_high, smoothing_low], axis=0)
 
     inverse = None
     weight_halves = None
@@ -388,13 +392,13 @@
                           r_mix.at[turn, 8 + x], plane(y - 1, other_x))
             far_copies.append((jnp.logical_and(above, other_x <= x), up))
             far_copies.append((jnp.logical_and(below, other_x >= x), down))
-        for step in range(1, LINE):
+        for needed, copy in far_copies:
+            pl.when(needed)(copy.start)
+        for step in (2, 1, 3):
             copy = remote(planes(2 * x, 2), planes(2 * x, 2), s_mix.at[turn, step - 1], r_mix.at[turn, x],
                           plane(y, lax.rem(x + step, LINE)))
             copy.start()
             line_copies.append(copy)
-        for needed, copy in far_copies:
-            pl.when(needed)(copy.start)
 
         for step in range(1, LINE):
             source_x = lax.rem(x + step, LINE)
@@ -407,12 +411,29 @@
                                 r_mix.at[turn, 4 + source_x], plane(y - 1, source_x))
             pl.when(jnp.logical_and(above, source_x <= x))(from_above.wait_recv)
             pl.when(jnp.logical_and(below, source_x >= x))(from_below.wait_recv)
-        summed = jnp.dot(smoothing, mixed[turn, :, :, 0:width].reshape(128, width),
-                         precision=lax.Precision.HIGHEST, preferred_element_type=F32)
+        high, low = split_two(mixed[turn, :, :, 0:width].reshape(128, width))
+        summed = jnp.dot(smoothing_both, high, preferred_element_type=F32)
+        summed = summed[0:16] + summed[16:32] + jnp.dot(smoothing_high, low, preferred_element_type=F32)
         if turn == 0:
             inverse = 1.0 / jnp.maximum(summed[:, 256:384], 1.0)
             inverse = jnp.concatenate([inverse, inverse], axis=1)
         gains_now = summed[:, 0:256] * inverse
+
+        if turn == ITERS - 1:
+            for z in range(2):
+                for channel in range(2):
+                    for row in range(8):
+                        half, lane, part = row // 4, (row // 2) % 2, row % 2
+                        at = z * 8 + half * 4 + part * 2 + channel
+                        stage[z, channel, row:row + 1, :] = gains_now[at:at + 1, lane * LANES:(lane + 1) * LANES]
+            gain_copies = []
+            for step in FAR_FIRST:
+                other, device = ring(step)
+                copy = remote(stage.at[lax.div(other, BL)], gains_out.at[:, me], s_gain.at[step], r_gain.at[step], device)
+                copy.start()
+                gain_copies.append(copy)
+            sends.extend(gain_copies)
+            gains_out[:, me] = stage[z_hi]
 
         put_ends(gains_now)
         for source in range(BL):
@@ -428,21 +449,6 @@
             copy.wait_send()
         for needed, copy in far_copies:
             pl.when(needed)(copy.wait_send)
-
-    for z in range(2):
-        for channel in range(2):
-            for row in range(8):
-                half, lane, part = row // 4, (row // 2) % 2, row % 2
-                at = z * 8 + half * 4 + part * 2 + channel
-                stage[z, channel, row:row + 1, :] = gains_now[at:at + 1, lane * LANES:(lane + 1) * LANES]
-    gain_copies = []
-    for step in range(1, RING):
-        other, device = ring(step)
-        copy = remote(stage.at[lax.div(other, BL)], gains_out.at[:, me], s_gain.at[step], r_gain.at[step], device)
-        copy.start()
-        gain_copies.append(copy)
-    sends.extend(gain_copies)
-    gains_out[:, me] = stage[z_hi]
 
     for copy in joint_copies:
         copy.wait_recv()
@@ -467,7 +473,7 @@
 
     gains, residual = pl.pallas_call(
         calibrate_kernel,
-        out_shape=(jax.ShapeDtypeStruct((2, DIRS, 8, LANES), F32), jax.ShapeDtypeStruct((64, LANES), F32)),
+        out_shape=(pltpu.VMEM((2, DIRS, 8, LANES), F32), pltpu.VMEM((64, LANES), F32)),
         in_specs=[anywhere, anywhere, vmem, vmem, vmem, vmem, smem, anywhere, anywhere, smem],
         out_specs=(vmem, vmem),
         scratch_shapes=[

time: 84.2 us -> 80.7 us (0.958)
  Pallas kernels: 81.2 us -> 78.6 us
  local copies, waits for them, and re-layouts: 2.19 us -> 1.27 us
    pallas_call x1, Pallas kernels: 81.2 us -> 78.6 us  [local(): pl.pallas_call(calibrate_kernel, out_shape=(pltpu.VMEM((2, DIRS, 8, LANES...]
    unnamed x4 -> x2, local copies, waits for them, and re-layouts: 2.19 us -> 1.27 us
where the time goes in v3:
time: 80.7 us; the launch traced here: 80.5 us
  Pallas kernels  78.6 us (97%)
  local copies, waits for them, and re-layouts  1.27 us (2%)
    pallas_call x1, Pallas kernels, local(): pl.pallas_call(calibrate_kernel, out_shape=(pltpu.VMEM((2, DIRS, 8, LANES...  78.6 us

profile of v3, /device:TPU:31, one launch (start us, length us, event | category | flops | bytes accessed | tf_op | source)
XLA Modules:
  0.0 80.5 jit_solution(18322177342834829197)
XLA Ops:
  0.6 78.6 %calibrate.1 = (f32[2,16,8,128]{3,2,1,0:T(8,128)S(1)}, f32[64,128]{1,0:T(8,128)S(1)}) custom-call(f32[64,128]{1,0:T(8,128)} %bitcast.21, f32[3,16,128]{2,1,0:T(8,128)} %coords_hbm.1, s32[2,128]{1,0:T(2,128)} %pair.1, f32[2,2,64]{2,1,0:T(2,128)} %position.1, f32[2,64]{1,0:T(2,128)} %flux.1, f32[2,64]{1,0:T(2,128)} %spectral.1, s32[2]{0:T(128)} %count.1, ...), custom_call_target="tpu_custom_call" | custom-call | tf_op jit(solution)/shard_map/calibrate/pallas_call | solution.py:474
  79.2 0.7 copy.17
  79.9 0.6 copy.18

commit v4 on v3

--- a/solution.py
+++ b/solution.py
@@ -11,7 +11,8 @@
 VMEM = pltpu.MemorySpace.VMEM
 SMEM = pltpu.MemorySpace.SMEM
 
-FAR_FIRST = (8, 7, 9, 6, 10, 5, 11, 4, 12, 3, 13, 2, 14, 1, 15)
+NEAR = (1, 15, 2, 14, 3, 13, 4, 12, 0)
+FAR = (8, 7, 9, 6, 10, 5, 11)
 BL = 8
 LINE = 4
 RING = 16
@@ -46,7 +47,10 @@
                      gains_out, residual_out,
                      noise, coords, true_gains, start_gains, params, ids, params_scalar, ids_scalar, running, model,
                      own_onehot, onehot, observed, joint_true, firsts, seconds, owned, first_out, first_in,
-                     energy, energy_in, fits, fits_in, joint_out, joint_in, mixed, stage,
+                     energy, energy_in, joint_start,
+                     fits_0, fits_1, fits_2, fits_3, fits_in_0, fits_in_1, fits_in_2, fits_in_3,
+                     joint_out_0, joint_out_1, joint_out_2, joint_out_3, joint_in_0, joint_in_1, joint_in_2, joint_in_3,
+                     mixed, stage,
                      s_load, s_param, r_param, s_ids, r_ids,
                      s_first, r_first, s_energy, r_energy, s_fit, r_fit, s_joint, r_joint,
                      s_mix, r_mix, s_gain, r_gain):
@@ -58,10 +62,19 @@
     me = z_hi * BL + bl
     above, below = y < lax.axis_size("freq") // 8 - 1, y > 0
 
+    z_lo, core = lax.div(bl, 2), lax.rem(bl, 2)
+    fits = (fits_0, fits_1, fits_2, fits_3)
+    fits_in = (fits_in_0, fits_in_1, fits_in_2, fits_in_3)
+    joint_out = (joint_out_0, joint_out_1, joint_out_2, joint_out_3)
+    joint_in = (joint_in_0, joint_in_1, joint_in_2, joint_in_3)
+    places = ((0, 0), (0, 1), (1, 0), (1, 1))
+
+    def ring_device(other):
+        return {"freq": (y * 2 + lax.div(other, BL)) * LINE + x, "bl": lax.rem(other, BL)}
+
     def ring(step):
         other = lax.rem(me + step, RING)
-        device = {"freq": (y * 2 + lax.div(other, BL)) * LINE + x, "bl": lax.rem(other, BL)}
-        return other, device
+        return other, ring_device(other)
 
     def plane(other_y, other_x):
         return {"freq": (other_y * 2 + z_hi) * LINE + other_x, "bl": bl}
@@ -133,13 +146,15 @@
         qr, qi = ends[0:32, LANES:], ends[32:64, LANES:]
         return pr * qr + pi * qi, pi * qr - pr * qi
 
-    for ref, gains in ((joint_true, true_gains), (joint_in.at[0], start_gains)):
+    for ref, gains in ((joint_true, true_gains), (joint_start, start_gains)):
         parts = local_joint(gains)
         for channel in range(2):
             for part in range(2):
                 for patch in range(DIRS):
                     at = channel * DIRS + patch
-                    ref[patch, part * 2 + channel:part * 2 + channel + 1, :] = parts[part][at:at + 1]
+                    offset = lax.rem((patch % BL) // 2 + LINE - z_lo, LINE)
+                    slot = (patch // BL) * 2 + patch % 2
+                    ref[offset, slot, part * 2 + channel:part * 2 + channel + 1, :] = parts[part][at:at + 1]
 
     away = (1 - z_hi) * BL + bl
     for channel in range(2):
@@ -216,20 +231,35 @@
 
     lax.fori_loop(0, DIRS, finish_patch, start, unroll=True)
 
-    def corrupted(joint, channel):
-        def add(patch, totals):
-            jr = joint[patch, channel:channel + 1, :]
-            ji = joint[patch, 2 + channel:3 + channel, :]
-            mr, mi = model[channel, patch, 0], model[channel, patch, 1]
-            return totals[0] + (jr * mr - ji * mi), totals[1] + (jr * mi + ji * mr)
-
-        zero = jnp.zeros((TIMES, LANES), F32)
-        return lax.fori_loop(0, DIRS, add, (zero, zero), unroll=True)
-
+    def chip_of(offset):
+        return lax.rem(z_lo + offset, LINE)
+
+    def corrupted(row, wait=None):
+        totals = [jnp.zeros((TIMES, LANES), F32) for _ in range(4)]
+        for offset in (2, 1, 3, 0):
+            if wait is not None:
+                wait(offset)
+            for slot, (z, which) in enumerate(places):
+                patch = z * BL + chip_of(offset) * 2 + which
+                for channel in range(2):
+                    jr, ji = row(offset, slot, channel), row(offset, slot, 2 + channel)
+                    mr, mi = model[channel, patch, 0], model[channel, patch, 1]
+                    totals[2 * channel] += jr * mr - ji * mi
+                    totals[2 * channel + 1] += jr * mi + ji * mr
+        return totals
+
+    def row_at_start(ref):
+        return lambda offset, slot, at: ref[offset, slot, at:at + 1, :]
+
+    def row_at(round_index):
+        if round_index == 0:
+            return row_at_start(joint_start)
+        return lambda offset, slot, at: joint_in[offset][round_index - 1, slot, at:at + 1, :]
+
+    totals = corrupted(row_at_start(joint_true))
     for channel in range(2):
-        totals = corrupted(joint_true, channel)
         for part in range(2):
-            observed[channel, part] = noise[pl.ds(channel * 32 + part, TIMES, stride=2), :] + totals[part]
+            observed[channel, part] = noise[pl.ds(channel * 32 + part, TIMES, stride=2), :] + totals[2 * channel + part]
 
     def put_energy(patch, _):
         for channel in range(2):
@@ -244,18 +274,43 @@
 
     lax.fori_loop(0, DIRS, put_energy, 0, unroll=True)
 
-    def to_ring(outgoing, incoming, send, recv):
-        copies = []
-        for step in FAR_FIRST:
-            other, device = ring(step)
-            copy = remote(outgoing.at[other], incoming.at[me], send.at[step], recv.at[step], device)
+    def ring_copy(src, dst, send, recv, other):
+        return remote(src, dst, send.at[other], recv.at[me], ring_device(other))
+
+    def send_ring(src, dst, send, recv, other):
+        copy = ring_copy(src, dst, send, recv, other)
+        copy.start()
+        sends.append(copy)
+
+    def wait_ring(landing, send, recv, other):
+        remote(landing, landing, send.at[other], recv.at[other], ring_device(other)).wait_recv()
+
+    def others_of(offset):
+        some = ((1 - z_hi, 0), (1 - z_hi, 1), (z_hi, 1 - core)) if offset == 0 else places
+        return [(z * 2 + which, z * BL + chip_of(offset) * 2 + which) for z, which in some]
+
+    own_slot = z_hi * 2 + core
+
+    def send_offset(outgoing, incoming, send, recv, turn, offset):
+        back = (LINE - offset) % LINE
+        for slot, other in others_of(offset):
+            copy = remote(outgoing[offset].at[turn, slot], incoming[back].at[turn, own_slot],
+                          send.at[turn, offset * 4 + slot], recv.at[turn, back * 4 + own_slot], ring_device(other))
             copy.start()
-            copies.append(copy)
-        incoming[me] = outgoing[me]
-        sends.extend(copies)
-        return copies
-
-    energy_copies = to_ring(energy, energy_in, s_energy, r_energy)
+            sends.append(copy)
+        if offset == 0:
+            incoming[0][turn, own_slot] = outgoing[0][turn, own_slot]
+
+    def wait_offset(incoming, send, recv, turn, offset):
+        for slot, other in others_of(offset):
+            landed = incoming[offset].at[turn, slot]
+            remote(landed, landed, send.at[turn, offset * 4 + slot], recv.at[turn, offset * 4 + slot],
+                   ring_device(other)).wait_recv()
+
+    for step in FAR + NEAR[:-1]:
+        other = ring(step)[0]
+        send_ring(energy.at[other], energy_in.at[me], s_energy, r_energy, other)
+    energy_in[me] = energy[me]
 
     row8 = lax.broadcasted_iota(jnp.int32, (8, LANES), 0)
     is_real = (row8 & 2) == 0
@@ -269,16 +324,23 @@
     def swapped(value):
         return jnp.where(is_real, from_later(value), from_earlier(value))
 
-    def put_ends(gains):
-        rows = jnp.concatenate([
+    def split_rows(gains):
+        return jnp.concatenate(split_two(jnp.concatenate([
             jnp.concatenate([gains[0:4], gains[8:12]], axis=0),
-            jnp.concatenate([gains[4:8], gains[12:16]], axis=0)], axis=1)
-        high, low = split_two(rows)
-        both = jnp.dot(jnp.concatenate([high, low], axis=0), onehot[...], preferred_element_type=F32)
+            jnp.concatenate([gains[4:8], gains[12:16]], axis=0)], axis=1)), axis=0)
+
+    def put_ends(rows, chip):
+        columns = onehot[:, pl.ds(pl.multiple_of(chip * 512, 512), 512)]
+        both = jnp.dot(rows, columns, preferred_element_type=F32)
         both = both[0:8] + both[8:16]
-        for source in range(BL):
-            firsts[source] = both[:, source * 256:source * 256 + LANES]
-            seconds[source] = both[:, source * 256 + LANES:source * 256 + 256]
+        pairs = []
+        for which in range(2):
+            start = which * 2 * LANES
+            near, far = both[:, start:start + LANES], both[:, start + LANES:start + 2 * LANES]
+            firsts[chip * 2 + which] = near
+            seconds[chip * 2 + which] = far
+            pairs.append((near, far))
+        return pairs
 
     def to_halves(rows):
         return jnp.concatenate([
@@ -294,37 +356,36 @@
     reached = jnp.where((here & 6) == (there & 6), jnp.where(jnp.abs(apart) <= REACH, 1.0, 0.0), 0.0)
     smoothing = jnp.exp(-(apart * apart) / (2.0 * SPREAD * SPREAD)) * reached
 
-    def fitted(round_index):
-        joint = joint_in.at[round_index]
-        for channel in range(2):
-            totals = corrupted(joint, channel)
-            rest_r = observed[channel, 0] - totals[0]
-            rest_i = observed[channel, 1] - totals[1]
-
-            def put_fit(patch, _):
-                mr, mi = model[channel, patch, 0], model[channel, patch, 1]
-                power = energy[patch, channel:channel + 1, :]
-                for part, value in enumerate((mr * rest_r + mi * rest_i, mr * rest_i - mi * rest_r)):
-                    at = part * 2 + channel
-                    row = jnp.sum(value, axis=0, keepdims=True)
-                    fits[round_index, patch, at:at + 1, :] = row + joint[patch, at:at + 1, :] * power
-                return 0
-
-            lax.fori_loop(0, DIRS, put_fit, 0, unroll=True)
-
     smoothing_high, smoothing_low = split_two(smoothing)
     smoothing_both = jnp.concatenate([smoothing_high, smoothing_low], axis=0)
+
+    def wait_joint(round_index):
+        if round_index == 0:
+            return None
+        return lambda offset: wait_offset(joint_in, s_joint, r_joint, round_index - 1, offset)
+
+    def fit_and_send(turn):
+        row = row_at(turn)
+        totals = corrupted(row, wait_joint(turn))
+        rests = [observed[place // 2, place % 2] - totals[place] for place in range(4)]
+        for offset in (0, 1, 3, 2):
+            for slot, (z, which) in enumerate(places):
+                patch = z * BL + chip_of(offset) * 2 + which
+                for channel in range(2):
+                    rest_r, rest_i = rests[2 * channel], rests[2 * channel + 1]
+                    mr, mi = model[channel, patch, 0], model[channel, patch, 1]
+                    power = energy[patch, channel:channel + 1, :]
+                    for part, value in enumerate((mr * rest_r + mi * rest_i, mr * rest_i - mi * rest_r)):
+                        at = part * 2 + channel
+                        fits[offset][turn, slot, at:at + 1, :] = (
+                            jnp.sum(value, axis=0, keepdims=True) + row(offset, slot, at) * power)
+            send_offset(fits, fits_in, s_fit, r_fit, turn, offset)
 
     inverse = None
     weight_halves = None
     weight_rows = None
-    power_rows = []
     for turn in range(ITERS):
-        if turn > 0:
-            for copy in joint_copies:
-                copy.wait_recv()
-        fitted(turn)
-        fit_copies = to_ring(fits.at[turn], fits_in.at[turn], s_fit.at[turn], r_fit.at[turn])
+        fit_and_send(turn)
         if turn == 0:
             for source in range(BL):
                 for end in range(2):
@@ -341,35 +402,39 @@
                     owned[z_hi, at:at + 1, lane * LANES:(lane + 1) * LANES] = own[row:row + 1]
                     owned[1 - z_hi, at:at + 1, lane * LANES:(lane + 1) * LANES] = other[row:row + 1]
             gains_now = owned[...].reshape(16, 256)
-            put_ends(gains_now)
-            for copy in energy_copies:
-                copy.wait_recv()
-            for source in range(BL):
-                power_rows.append(jnp.concatenate([energy_in[source, 0:4], energy_in[BL + source, 0:4]], axis=0))
+            rows = split_rows(gains_now)
+            for chip in range(LINE):
+                put_ends(rows, chip)
+            for step in NEAR[:-1] + FAR:
+                other = ring(step)[0]
+                wait_ring(energy_in.at[other], s_energy, r_energy, other)
             weight_rows = jnp.concatenate([energy_in[0, 4:8], energy_in[BL, 4:8]], axis=0)
             weight_rows = jnp.concatenate([weight_rows] * 4, axis=1)
             weight_halves = to_halves(weight_rows)
-        for copy in fit_copies:
-            copy.wait_recv()
-
-        columns = []
-        for source in range(BL):
-            fit = jnp.concatenate([fits_in[turn, source], fits_in[turn, BL + source]], axis=0)
-            power = power_rows[source]
-            for toward_first in (True, False):
-                far = (seconds if toward_first else firsts)[source]
-                far_swapped = swapped(far)
-                direct = far * fit
-                crossed = far_swapped * fit
-                if toward_first:
-                    numer = jnp.where(is_real, direct - from_later(direct), crossed + from_earlier(crossed))
-                else:
-                    numer = jnp.where(is_real, direct + from_later(direct), from_earlier(crossed) - crossed)
-                denom = (far * far + far_swapped * far_swapped) * power
-                high, low = split_two(jnp.concatenate([numer, denom], axis=0))
-                columns.append(jnp.concatenate([high, low], axis=0))
-        received = lax.dot_general(
-            jnp.concatenate(columns, axis=1), onehot[...], (((1,), (1,)), ((), ())), preferred_element_type=F32)
+
+        received = jnp.zeros((32, STATIONS), F32)
+        for offset in (2, 1, 3, 0):
+            chip = chip_of(offset)
+            wait_offset(fits_in, s_fit, r_fit, turn, offset)
+            columns = []
+            for which in range(2):
+                source = chip * 2 + which
+                fit = jnp.concatenate([fits_in[offset][turn, which], fits_in[offset][turn, 2 + which]], axis=0)
+                power = jnp.concatenate([energy_in[source, 0:4], energy_in[BL + source, 0:4]], axis=0)
+                for toward_first in (True, False):
+                    far = (seconds if toward_first else firsts)[source]
+                    far_swapped = swapped(far)
+                    direct = far * fit
+                    crossed = far_swapped * fit
+                    if toward_first:
+                        numer = jnp.where(is_real, direct - from_later(direct), crossed + from_earlier(crossed))
+                    else:
+                        numer = jnp.where(is_real, direct + from_later(direct), from_earlier(crossed) - crossed)
+                    denom = (far * far + far_swapped * far_swapped) * power
+                    columns.append(jnp.concatenate(split_two(jnp.concatenate([numer, denom], axis=0)), axis=0))
+            received = received + lax.dot_general(
+                jnp.concatenate(columns, axis=1), onehot[:, pl.ds(pl.multiple_of(chip * 512, 512), 512)],
+                (((1,), (1,)), ((), ())), preferred_element_type=F32)
         received = received[0:16] + received[16:32]
         solved = (received[0:8] * weight_rows) / jnp.maximum(received[8:16] * weight_rows, 1.0)
         blended = 0.5 * gains_now + 0.5 * to_halves(solved)
@@ -426,38 +491,35 @@
                         half, lane, part = row // 4, (row // 2) % 2, row % 2
                         at = z * 8 + half * 4 + part * 2 + channel
                         stage[z, channel, row:row + 1, :] = gains_now[at:at + 1, lane * LANES:(lane + 1) * LANES]
-            gain_copies = []
-            for step in FAR_FIRST:
-                other, device = ring(step)
-                copy = remote(stage.at[lax.div(other, BL)], gains_out.at[:, me], s_gain.at[step], r_gain.at[step], device)
-                copy.start()
-                gain_copies.append(copy)
-            sends.extend(gain_copies)
+            for step in FAR + NEAR[:-1]:
+                other = ring(step)[0]
+                send_ring(stage.at[lax.div(other, BL)], gains_out.at[:, me], s_gain, r_gain, other)
             gains_out[:, me] = stage[z_hi]
 
-        put_ends(gains_now)
-        for source in range(BL):
-            near, far = firsts[source], seconds[source]
-            direct = near * far
-            crossed = near * swapped(far)
-            joint = jnp.where(is_real, direct + from_later(direct), crossed - from_earlier(crossed))
-            joint_out[turn, source] = joint[0:4]
-            joint_out[turn, BL + source] = joint[4:8]
-        joint_copies = to_ring(joint_out.at[turn], joint_in.at[turn + 1], s_joint.at[turn], r_joint.at[turn])
+        rows = split_rows(gains_now)
+        for offset in (0, 1, 3, 2):
+            chip = chip_of(offset)
+            for which, (near, far) in enumerate(put_ends(rows, chip)):
+                direct = near * far
+                crossed = near * swapped(far)
+                joint = jnp.where(is_real, direct + from_later(direct), crossed - from_earlier(crossed))
+                joint_out[offset][turn, which] = joint[0:4]
+                joint_out[offset][turn, 2 + which] = joint[4:8]
+            send_offset(joint_out, joint_in, s_joint, r_joint, turn, offset)
 
         for copy in line_copies:
             copy.wait_send()
         for needed, copy in far_copies:
             pl.when(needed)(copy.wait_send)
 
-    for copy in joint_copies:
-        copy.wait_recv()
+    totals = corrupted(row_at(ITERS), wait_joint(ITERS))
     for channel in range(2):
-        totals = corrupted(joint_in.at[ITERS], channel)
         for part in range(2):
-            residual_out[pl.ds(channel * 32 + part, TIMES, stride=2), :] = observed[channel, part] - totals[part]
-    for copy in gain_copies:
-        copy.wait_recv()
+            residual_out[pl.ds(channel * 32 + part, TIMES, stride=2), :] = (
+                observed[channel, part] - totals[2 * channel + part])
+    for step in NEAR[:-1] + FAR:
+        other = ring(step)[0]
+        wait_ring(gains_out.at[:, other], s_gain, r_gain, other)
     for copy in sends:
         copy.wait_send()
 
@@ -490,7 +552,7 @@
             pltpu.VMEM((STATIONS, 2 * LANES), BF16),
             pltpu.VMEM((STATIONS, BL * 2 * LANES), BF16),
             pltpu.VMEM((2, 2, TIMES, LANES), F32),
-            pltpu.VMEM((DIRS, 4, LANES), F32),
+            pltpu.VMEM((LINE, 4, 4, LANES), F32),
             pltpu.VMEM((BL, 8, LANES), F32),
             pltpu.VMEM((BL, 8, LANES), F32),
             pltpu.VMEM((2, 8, 256), F32),
@@ -498,10 +560,8 @@
             pltpu.VMEM((2, 8, LANES), F32),
             pltpu.VMEM((RING, 8, LANES), F32),
             pltpu.VMEM((RING, 8, LANES), F32),
-            pltpu.VMEM((ITERS, RING, 4, LANES), F32),
-            pltpu.VMEM((ITERS, RING, 4, LANES), F32),
-            pltpu.VMEM((ITERS, RING, 4, LANES), F32),
-            pltpu.VMEM((ITERS + 1, RING, 4, LANES), F32),
+            pltpu.VMEM((LINE, 4, 4, LANES), F32),
+        ] + [pltpu.VMEM((ITERS, 4, 4, LANES), F32)] * 16 + [
             pltpu.VMEM((ITERS, 16, 8, 384), F32),
             pltpu.VMEM((2, 2, 8, LANES), F32),
             dma((6,)), dma((BL,)), dma((BL,)), dma((BL,)), dma((BL,)),

time: 80.7 us -> 78.4 us (0.971)
  Pallas kernels: 78.6 us -> 76.3 us
    pallas_call x1, Pallas kernels: 78.6 us -> 76.3 us  [local(): pl.pallas_call(calibrate_kernel, out_shape=(pltpu.VMEM((2, DIRS, 8, LANES...]
where the time goes in v4:
time: 78.4 us; the launch traced here: 78.3 us
  Pallas kernels  76.3 us (97%)
  local copies, waits for them, and re-layouts  1.27 us (2%)
    pallas_call x1, Pallas kernels, local(): pl.pallas_call(calibrate_kernel, out_shape=(pltpu.VMEM((2, DIRS, 8, LANES...  76.3 us

profile of v4, /device:TPU:31, one launch (start us, length us, event | category | flops | bytes accessed | tf_op | source)
XLA Modules:
  0.0 78.3 jit_solution(16210731797709440246)
XLA Ops:
  0.6 76.3 %calibrate.1 = (f32[2,16,8,128]{3,2,1,0:T(8,128)S(1)}, f32[64,128]{1,0:T(8,128)S(1)}) custom-call(f32[64,128]{1,0:T(8,128)} %bitcast.21, f32[3,16,128]{2,1,0:T(8,128)} %coords_hbm.1, s32[2,128]{1,0:T(2,128)} %pair.1, f32[2,2,64]{2,1,0:T(2,128)} %position.1, f32[2,64]{1,0:T(2,128)} %flux.1, f32[2,64]{1,0:T(2,128)} %spectral.1, s32[2]{0:T(128)} %count.1, ...), custom_call_target="tpu_custom_call" | custom-call | tf_op jit(solution)/shard_map/calibrate/pallas_call | solution.py:536
  77.0 0.7 copy.17
  77.6 0.6 copy.18

commit v5 on v4

--- a/solution.py
+++ b/solution.py
@@ -45,12 +45,12 @@
 
 def calibrate_kernel(noise_hbm, coords_hbm, pair, position, flux, spectral, count, true_hbm, start_hbm, flags,
                      gains_out, residual_out,
-                     noise, coords, true_gains, start_gains, params, ids, params_scalar, ids_scalar, running, model,
+                     noise, coords, true_gains, start_gains, params, ids, counts, params_scalar, counts_scalar, running, model,
                      own_onehot, onehot, observed, joint_true, firsts, seconds, owned, first_out, first_in,
                      energy, energy_in, joint_start,
                      fits_0, fits_1, fits_2, fits_3, fits_in_0, fits_in_1, fits_in_2, fits_in_3,
                      joint_out_0, joint_out_1, joint_out_2, joint_out_3, joint_in_0, joint_in_1, joint_in_2, joint_in_3,
-                     mixed, stage,
+                     mixed, mixed_far, stage,
                      s_load, s_param, r_param, s_ids, r_ids,
                      s_first, r_first, s_energy, r_energy, s_fit, r_fit, s_joint, r_joint,
                      s_mix, r_mix, s_gain, r_gain):
@@ -86,7 +86,7 @@
         copy.start()
         loads.append(copy)
 
-    mixed[...] = jnp.zeros(mixed.shape, F32)
+    mixed_far[...] = jnp.zeros(mixed_far.shape, F32)
 
     barrier = pltpu.get_barrier_semaphore()
     for step in range(1, RING):
@@ -182,8 +182,10 @@
     sends.append(first_copy)
     for copy in param_copies:
         copy.wait_recv()
-    scalars = [pltpu.make_async_copy(params, params_scalar, s_load.at[4]),
-               pltpu.make_async_copy(ids, ids_scalar, s_load.at[5])]
+    for device in range(BL):
+        counts[device:device + 1, :] = ids[device, 2:3, :]
+    scalars = [pltpu.make_async_copy(counts, counts_scalar, s_load.at[4]),
+               pltpu.make_async_copy(params, params_scalar, s_load.at[5])]
     for copy in scalars:
         copy.start()
     for copy in scalars:
@@ -194,7 +196,7 @@
     u, v, w = coords[0] * ratio_zero, coords[1] * ratio_zero, coords[2] * ratio_zero
 
     def lives_of(patch):
-        return ids_scalar[patch >> 1, 2, patch & 1]
+        return counts_scalar[patch >> 1, patch & 1]
 
     def one_component(component, state):
         sums, (patch, slot, live) = list(state[0:4]), state[4:7]
@@ -218,7 +220,7 @@
 
     zero = jnp.zeros((TIMES, LANES), F32)
     start = jnp.int32(0)
-    lax.fori_loop(0, COMPONENTS, one_component, (zero,) * 4 + (start, start, lives_of(start)), unroll=16)
+    lax.fori_loop(0, COMPONENTS, one_component, (zero,) * 4 + (start, start, lives_of(start)), unroll=32)
 
     def finish_patch(patch, end):
         end = end + lives_of(patch)
@@ -307,10 +309,6 @@
             remote(landed, landed, send.at[turn, offset * 4 + slot], recv.at[turn, offset * 4 + slot],
                    ring_device(other)).wait_recv()
 
-    for step in FAR + NEAR[:-1]:
-        other = ring(step)[0]
-        send_ring(energy.at[other], energy_in.at[me], s_energy, r_energy, other)
-    energy_in[me] = energy[me]
 
     row8 = lax.broadcasted_iota(jnp.int32, (8, LANES), 0)
     is_real = (row8 & 2) == 0
@@ -387,6 +385,10 @@
     for turn in range(ITERS):
         fit_and_send(turn)
         if turn == 0:
+            for step in FAR + NEAR[:-1]:
+                other = ring(step)[0]
+                send_ring(energy.at[other], energy_in.at[me], s_energy, r_energy, other)
+            energy_in[me] = energy[me]
             for source in range(BL):
                 for end in range(2):
                     row = ids[source, end:end + 1, :]
@@ -449,11 +451,14 @@
         def planes(first, count):
             return mixed.at[turn, pl.ds(first, count), :, pl.ds(0, width)]
 
+        def far_plane(index):
+            return mixed_far.at[turn, pl.ds(index, 1), :, pl.ds(0, width)]
+
         line_copies, far_copies = [], []
         for other_x in range(LINE):
-            up = remote(planes(2 * x + 1, 1), planes(8 + x, 1), s_mix.at[turn, 3 + other_x],
+            up = remote(planes(2 * x + 1, 1), far_plane(x), s_mix.at[turn, 3 + other_x],
                         r_mix.at[turn, 4 + x], plane(y + 1, other_x))
-            down = remote(planes(2 * x, 1), planes(12 + x, 1), s_mix.at[turn, 7 + other_x],
+            down = remote(planes(2 * x, 1), far_plane(4 + x), s_mix.at[turn, 7 + other_x],
                           r_mix.at[turn, 8 + x], plane(y - 1, other_x))
             far_copies.append((jnp.logical_and(above, other_x <= x), up))
             far_copies.append((jnp.logical_and(below, other_x >= x), down))
@@ -469,21 +474,27 @@
             source_x = lax.rem(x + step, LINE)
             remote(planes(2 * source_x, 2), planes(2 * source_x, 2), s_mix.at[turn, step - 1],
                    r_mix.at[turn, source_x], plane(y, source_x)).wait_recv()
+
+        def smoothed(planes_now, first):
+            high, low = split_two(planes_now[turn, :, :, 0:width].reshape(64, width))
+            both = jnp.dot(smoothing_both[:, first:first + 64], high, preferred_element_type=F32)
+            return both[0:16] + both[16:32] + jnp.dot(smoothing_high[:, first:first + 64], low, preferred_element_type=F32)
+
+        summed = smoothed(mixed, 0)
         for source_x in range(LINE):
-            from_above = remote(planes(12 + source_x, 1), planes(12 + source_x, 1), s_mix.at[turn, 3 + source_x],
+            from_above = remote(far_plane(4 + source_x), far_plane(4 + source_x), s_mix.at[turn, 3 + source_x],
                                 r_mix.at[turn, 8 + source_x], plane(y + 1, source_x))
-            from_below = remote(planes(8 + source_x, 1), planes(8 + source_x, 1), s_mix.at[turn, 7 + source_x],
+            from_below = remote(far_plane(source_x), far_plane(source_x), s_mix.at[turn, 7 + source_x],
                                 r_mix.at[turn, 4 + source_x], plane(y - 1, source_x))
             pl.when(jnp.logical_and(above, source_x <= x))(from_above.wait_recv)
             pl.when(jnp.logical_and(below, source_x >= x))(from_below.wait_recv)
-        high, low = split_two(mixed[turn, :, :, 0:width].reshape(128, width))
-        summed = jnp.dot(smoothing_both, high, preferred_element_type=F32)
-        summed = summed[0:16] + summed[16:32] + jnp.dot(smoothing_high, low, preferred_element_type=F32)
+        summed = summed + smoothed(mixed_far, 64)
         if turn == 0:
             inverse = 1.0 / jnp.maximum(summed[:, 256:384], 1.0)
             inverse = jnp.concatenate([inverse, inverse], axis=1)
         gains_now = summed[:, 0:256] * inverse
 
+        earlier = len(sends)
         if turn == ITERS - 1:
             for z in range(2):
                 for channel in range(2):
@@ -506,6 +517,9 @@
                 joint_out[offset][turn, which] = joint[0:4]
                 joint_out[offset][turn, 2 + which] = joint[4:8]
             send_offset(joint_out, joint_in, s_joint, r_joint, turn, offset)
+        if turn == ITERS - 1:
+            for copy in sends[:earlier]:
+                copy.wait_send()
 
         for copy in line_copies:
             copy.wait_send()
@@ -520,7 +534,7 @@
     for step in NEAR[:-1] + FAR:
         other = ring(step)[0]
         wait_ring(gains_out.at[:, other], s_gain, r_gain, other)
-    for copy in sends:
+    for copy in sends[earlier:]:
         copy.wait_send()
 
 
@@ -545,8 +559,9 @@
             pltpu.VMEM((256, LANES), F32),
             pltpu.VMEM((BL, 8, LANES), F32),
             pltpu.VMEM((BL, 8, LANES), jnp.int32),
+            pltpu.VMEM((BL, LANES), jnp.int32),
             pltpu.SMEM((BL, 8, LANES), F32),
-            pltpu.SMEM((BL, 8, LANES), jnp.int32),
+            pltpu.SMEM((BL, LANES), jnp.int32),
             pltpu.VMEM((COMPONENTS, 4, TIMES, LANES), F32),
             pltpu.VMEM((2, DIRS, 2, TIMES, LANES), F32),
             pltpu.VMEM((STATIONS, 2 * LANES), BF16),
@@ -562,7 +577,8 @@
             pltpu.VMEM((RING, 8, LANES), F32),
             pltpu.VMEM((LINE, 4, 4, LANES), F32),
         ] + [pltpu.VMEM((ITERS, 4, 4, LANES), F32)] * 16 + [
-            pltpu.VMEM((ITERS, 16, 8, 384), F32),
+            pltpu.VMEM((ITERS, 8, 8, 384), F32),
+            pltpu.VMEM((ITERS, 8, 8, 384), F32),
             pltpu.VMEM((2, 2, 8, LANES), F32),
             dma((6,)), dma((BL,)), dma((BL,)), dma((BL,)), dma((BL,)),
             dma(()), dma(()),

time: 78.4 us -> 77.8 us (level)
  no operation moved by 1% of the time
where the time goes in v5:
time: 77.8 us; the launch traced here: 77.7 us
  Pallas kernels  75.8 us (97%)
  local copies, waits for them, and re-layouts  1.27 us (2%)
    pallas_call x1, Pallas kernels, local(): pl.pallas_call(calibrate_kernel, out_shape=(pltpu.VMEM((2, DIRS, 8, LANES...  75.8 us

profile of v5, /device:TPU:31, one launch (start us, length us, event | category | flops | bytes accessed | tf_op | source)
XLA Modules:
  0.0 77.7 jit_solution(15786157771994969738)
XLA Ops:
  0.6 75.8 %calibrate.1 = (f32[2,16,8,128]{3,2,1,0:T(8,128)S(1)}, f32[64,128]{1,0:T(8,128)S(1)}) custom-call(f32[64,128]{1,0:T(8,128)} %bitcast.21, f32[3,16,128]{2,1,0:T(8,128)} %coords_hbm.1, s32[2,128]{1,0:T(2,128)} %pair.1, f32[2,2,64]{2,1,0:T(2,128)} %position.1, f32[2,64]{1,0:T(2,128)} %flux.1, f32[2,64]{1,0:T(2,128)} %spectral.1, s32[2]{0:T(128)} %count.1, ...), custom_call_target="tpu_custom_call" | custom-call | tf_op jit(solution)/shard_map/calibrate/pallas_call | solution.py:550
  76.4 0.7 copy.17
  77.1 0.6 copy.18

commit v6 on v5

--- a/solution.py
+++ b/solution.py
@@ -47,7 +47,7 @@
                      gains_out, residual_out,
                      noise, coords, true_gains, start_gains, params, ids, counts, params_scalar, counts_scalar, running, model,
                      own_onehot, onehot, observed, joint_true, firsts, seconds, owned, first_out, first_in,
-                     energy, energy_in, joint_start,
+                     energy, energy_in, joint_start, joint_apart,
                      fits_0, fits_1, fits_2, fits_3, fits_in_0, fits_in_1, fits_in_2, fits_in_3,
                      joint_out_0, joint_out_1, joint_out_2, joint_out_3, joint_in_0, joint_in_1, joint_in_2, joint_in_3,
                      mixed, mixed_far, stage,
@@ -146,8 +146,9 @@
         qr, qi = ends[0:32, LANES:], ends[32:64, LANES:]
         return pr * qr + pi * qi, pi * qr - pr * qi
 
-    for ref, gains in ((joint_true, true_gains), (joint_start, start_gains)):
-        parts = local_joint(gains)
+    true_parts, start_parts = local_joint(true_gains), local_joint(start_gains)
+    apart_parts = [true_parts[part] - start_parts[part] for part in range(2)]
+    for ref, parts in ((joint_true, true_parts), (joint_start, start_parts), (joint_apart, apart_parts)):
         for channel in range(2):
             for part in range(2):
                 for patch in range(DIRS):
@@ -258,11 +259,6 @@
             return row_at_start(joint_start)
         return lambda offset, slot, at: joint_in[offset][round_index - 1, slot, at:at + 1, :]
 
-    totals = corrupted(row_at_start(joint_true))
-    for channel in range(2):
-        for part in range(2):
-            observed[channel, part] = noise[pl.ds(channel * 32 + part, TIMES, stride=2), :] + totals[2 * channel + part]
-
     def put_energy(patch, _):
         for channel in range(2):
             mr, mi = model[channel, patch, 0], model[channel, patch, 1]
@@ -364,8 +360,12 @@
 
     def fit_and_send(turn):
         row = row_at(turn)
-        totals = corrupted(row, wait_joint(turn))
-        rests = [observed[place // 2, place % 2] - totals[place] for place in range(4)]
+        if turn == 0:
+            totals = corrupted(row_at_start(joint_apart))
+            rests = [noise[pl.ds((place // 2) * 32 + place % 2, TIMES, stride=2), :] + totals[place] for place in range(4)]
+        else:
+            totals = corrupted(row, wait_joint(turn))
+            rests = [observed[place // 2, place % 2] - totals[place] for place in range(4)]
         for offset in (0, 1, 3, 2):
             for slot, (z, which) in enumerate(places):
                 patch = z * BL + chip_of(offset) * 2 + which
@@ -389,6 +389,10 @@
                 other = ring(step)[0]
                 send_ring(energy.at[other], energy_in.at[me], s_energy, r_energy, other)
             energy_in[me] = energy[me]
+            totals = corrupted(row_at_start(joint_true))
+            for channel in range(2):
+                for part in range(2):
+                    observed[channel, part] = noise[pl.ds(channel * 32 + part, TIMES, stride=2), :] + totals[2 * channel + part]
             for source in range(BL):
                 for end in range(2):
                     row = ids[source, end:end + 1, :]
@@ -576,6 +580,7 @@
             pltpu.VMEM((RING, 8, LANES), F32),
             pltpu.VMEM((RING, 8, LANES), F32),
             pltpu.VMEM((LINE, 4, 4, LANES), F32),
+            pltpu.VMEM((LINE, 4, 4, LANES), F32),
         ] + [pltpu.VMEM((ITERS, 4, 4, LANES), F32)] * 16 + [
             pltpu.VMEM((ITERS, 8, 8, 384), F32),
             pltpu.VMEM((ITERS, 8, 8, 384), F32),

time: 77.8 us -> 77.7 us (level)
  no operation moved by 1% of the time
where the time goes in v6:
time: 77.7 us; the launch traced here: 77.6 us
  Pallas kernels  75.7 us (97%)
  local copies, waits for them, and re-layouts  1.27 us (2%)
    pallas_call x1, Pallas kernels, local(): pl.pallas_call(calibrate_kernel, out_shape=(pltpu.VMEM((2, DIRS, 8, LANES...  75.7 us

profile of v6, /device:TPU:31, one launch (start us, length us, event | category | flops | bytes accessed | tf_op | source)
XLA Modules:
  0.0 77.6 jit_solution(12298033007960010853)
XLA Ops:
  0.6 75.7 %calibrate.1 = (f32[2,16,8,128]{3,2,1,0:T(8,128)S(1)}, f32[64,128]{1,0:T(8,128)S(1)}) custom-call(f32[64,128]{1,0:T(8,128)} %bitcast.21, f32[3,16,128]{2,1,0:T(8,128)} %coords_hbm.1, s32[2,128]{1,0:T(2,128)} %pair.1, f32[2,2,64]{2,1,0:T(2,128)} %position.1, f32[2,64]{1,0:T(2,128)} %flux.1, f32[2,64]{1,0:T(2,128)} %spectral.1, s32[2]{0:T(128)} %count.1, ...), custom_call_target="tpu_custom_call" | custom-call | tf_op jit(solution)/shard_map/calibrate/pallas_call | solution.py:554
  76.3 0.7 copy.17
  77.0 0.6 copy.18
